TPU v7x, 256 devices: a whole 4x4x8 slice. The times are simulated.
256 devices in a mesh: blk: 16 (over z, y_hi), labels: 16 (over x, y_lo, core).
Axes of the slice: x: 4, y: 4 (y_hi: 2, y_lo: 2; y = y_hi * 2 + y_lo), z: 8, core: 2. Of those that a mesh axis runs over, the one named last changes fastest.
Arguments:
- features: bfloat16 [12288, 4096], P('blk'), may hold values from -0.099609375 to 0.099609375
- positives: int32 [12288, 8], P('blk'), may hold values from 0 to 131071
- tile_rows: int32 [1024, 4], P(('labels', 'blk')), may hold values from 0 to 31, as said below
- tile_count: int32 [1024], P(('labels', 'blk')), may hold values from 1 to 4, as said below
- weight: float32 [1024, 4, 128, 128], P(('labels', 'blk')), may hold values from -96 to 96
- first_moment: float32 [1024, 4, 128, 128], P(('labels', 'blk')), may hold values from -3 to 3
- second_moment: float32 [1024, 4, 128, 128], P(('labels', 'blk')), may hold values from 0.05 to 2
Outputs:
- new_weight: float32 [1024, 4, 128, 128], P(('labels', 'blk'))
- new_first: float32 [1024, 4, 128, 128], P(('labels', 'blk'))
- new_second: float32 [1024, 4, 128, 128], P(('labels', 'blk'))
Inputs may be any that keep to these rules, and one draw needn't show every extreme that they name: `tile_rows`: in each column block the 4 entries are distinct tile rows; only the first tile_count entries name kept tiles. `tile_count`: every column block keeps at least one tile.
All inputs are finite; a program needn't handle non-finite values.
Results may differ from a plain program's by a relative error of at most 0.0003.
Values may be sent and summed in bfloat16 or wider, within the bound.
No kernel may reach another device: no remote copies, remote signals or barrier semaphores. Data moves between devices by JAX's collectives and lax.ppermute only.
A program may use at most 64 MiB of HBM per device.

v0:
```python
import jax
import jax.numpy as jnp
from jax import lax
from jax.sharding import PartitionSpec as P

beta_one = 0.9
beta_two = 0.999
adam_eps = 1e-08
learn_rate = 0.1
correction_one = 1.0 - 0.9**10
correction_two = 1.0 - 0.999**10


def from_behind(array, axis, by):
    devices = lax.axis_size(axis)
    return lax.ppermute(array, axis, [(i, (i + by) % devices) for i in range(devices)])


def tile_residual(chosen, positives, block_count, block_tiles, block_base):
    tile_side = block_tiles.shape[-1]
    slot_ids = jnp.arange(block_tiles.shape[0], dtype=jnp.int32)
    live_mask = slot_ids < block_count
    w_masked = jnp.where(live_mask[:, None, None], block_tiles, jnp.zeros_like(block_tiles))
    logits = jnp.einsum("rsk,skt->rt", chosen, w_masked, preferred_element_type=jnp.float32)
    label_ids = block_base + jnp.arange(tile_side, dtype=jnp.int32)
    targets = jnp.any(positives[:, :, None] == label_ids[None, None, :], axis=1).astype(jnp.float32)
    return (jax.nn.sigmoid(logits) - targets).astype(jnp.bfloat16)


def block_both(tile_split, positives, row_ids, slot_counts, tiles_now, label_base):

    def one_block(block_args):
        block_rows, block_count, block_tiles, block_base = block_args
        chosen = jnp.take(tile_split, block_rows, axis=1)
        block_resid = tile_residual(chosen, positives, block_count, block_tiles, block_base)
        return jnp.einsum("rsk,rt->skt", chosen, block_resid, preferred_element_type=jnp.float32)

    return lax.map(one_block, (row_ids, slot_counts, tiles_now, label_base))


def local(features, positives, tile_rows, tile_count, weight, first_moment, second_moment):
    own_blocks = weight.shape[0]
    tile_side = weight.shape[-1]
    row_total = features.shape[0]
    tile_split = features.reshape(row_total, features.shape[1] // tile_side, tile_side)
    all_rows, all_counts = (
        lax.all_gather(tile_rows, "blk", axis=0, tiled=True),
        lax.all_gather(tile_count, "blk", axis=0, tiled=True),
    )
    group_blocks = all_rows.shape[0]
    group_base = lax.axis_index("labels") * (group_blocks * tile_side)
    tiles_half = weight.astype(jnp.bfloat16)

    def slice_index(first_row, block_total):
        row_ids = lax.dynamic_slice_in_dim(all_rows, first_row, block_total, 0)
        slot_counts = lax.dynamic_slice_in_dim(all_counts, first_row, block_total, 0)
        label_base = group_base + (first_row + jnp.arange(block_total, dtype=jnp.int32)) * tile_side
        return (row_ids, slot_counts, label_base)

    cycle_pos = lax.axis_index("blk")
    cycle_size = lax.axis_size("blk")

    def turn(turn_idx, loop_state):
        tiles_now, accumulated = loop_state
        owner_idx = jnp.mod(cycle_pos - turn_idx, cycle_size)
        first_row = owner_idx * own_blocks
        row_ids, slot_counts, label_base = slice_index(first_row, own_blocks)
        accumulated = accumulated + block_both(
            tile_split, positives, row_ids, slot_counts, tiles_now, label_base
        )
        tiles_now = from_behind(tiles_now, "blk", 1)
        accumulated = from_behind(accumulated, "blk", 1)
        return (tiles_now, accumulated)

    start_acc = jnp.zeros(weight.shape, jnp.float32)
    _, gradient = lax.fori_loop(0, cycle_size, turn, (tiles_half, start_acc))
    slot_ids = jnp.arange(weight.shape[1], dtype=jnp.int32)
    kept = (slot_ids[None, :] < tile_count[:, None])[:, :, None, None]
    moved_first = beta_one * first_moment + (1.0 - beta_one) * gradient
    moved_second = beta_two * second_moment + (1.0 - beta_two) * gradient * gradient
    step_dir = moved_first / correction_one / (jnp.sqrt(moved_second / correction_two) + adam_eps)
    moved_weight = weight - learn_rate * step_dir
    new_weight = jnp.where(kept, moved_weight, weight)
    new_first = jnp.where(kept, moved_first, first_moment)
    new_second = jnp.where(kept, moved_second, second_moment)
    return (new_weight, new_first, new_second)


def solution(mesh):
    return jax.shard_map(
        local,
        mesh=mesh,
        in_specs=(
            P("blk", None),
            P("blk", None),
            P(("labels", "blk"), None),
            P(("labels", "blk")),
            P(("labels", "blk"), None, None, None),
            P(("labels", "blk"), None, None, None),
            P(("labels", "blk"), None, None, None),
        ),
        out_specs=(
            P(("labels", "blk"), None, None, None),
            P(("labels", "blk"), None, None, None),
            P(("labels", "blk"), None, None, None),
        ),
        check_vma=False,
    )
```

profile of v0, /device:TPU:4, one launch (start us, length us, event | category | flops | bytes accessed | tf_op | source)
XLA Modules:
  0.0 1296.5 jit_solution(11238380679890569578)
XLA Ops:
  3.4 20.2 %all-reduce = s32[64]{0:T(128)S(1)} all-reduce(s32[64]{0:T(128)S(1)} %dynamic-update-slice), channel_id=1, replica_groups=mesh['blk'=16,'labels'=16] {'blk'}, use_global_device_ids=true, to_apply=%add | all-reduce | flops 64 | bytes 512
  23.6 8.6 copy.23
  32.3 8.7 copy.24
  41.3 38.9 %all-gather = s32[16,4,4]{2,1,0:T(4,128)S(1)} all-gather(s32[1,4,4]{2,1,0:T(4,128)S(1)} %bitcast.70), channel_id=1, replica_groups=mesh['blk'=16,'labels'=16] {'blk'}, dimensions={0}, use_global_device_ids=true | all-gather | bytes 1088 | tf_op jit(solution)/shard_map/all_gather | solution.py:47
  80.3 1211.6 %while.49 = (s32[]{:T(128)}, bf16[4,4,128,128]{3,2,1,0:T(8,128)(2,1)S(1)}, f32[4,4,128,128]{3,2,1,0:T(8,128)S(1)}, s32[]{:T(128)}, s32[64,4]{1,0:T(8,128)S(1)}, ...) while((s32[]{:T(128)}, ...), condition=%wide.region_4.5_spmd, body=%wide.region_0.4_spmd.sunk | while | flops 204506320 | bytes 14254457 | solution.py:76
  81.2 48.6 %while.50 = (s32[]{:T(128)}, f32[4,4,128,128]{3,2,1,0:T(8,128)S(1)}, s32[4,4]{1,0:T(4,128)S(1)}, bf16[768,32,128]{2,0,1:T(8,128)(2,1)}, s32[4]{0:T(128)S(1)}, /*...) while((s32[]{:T(128)}, f32[4,4,128,128]{3,2,1,0:T(8,128)S(1)}, ...), condition=%wide.region_3.3_spmd, body=%wide.region_1.2_spmd.sunk | while | flops 204244144 | bytes 3768029 | solution.py:38
  87.5 3.9 compare_reduce_fusion.2
  99.6 3.9 compare_reduce_fusion.2
  123.9 3.9 compare_reduce_fusion.2
  133.2 26.6 %collective-permute-done = bf16[4,4,128,128]{3,2,1,0:T(8,128)(2,1)S(1)} collective-permute-done((bf16[4,4,128,128]{3,2,1,0:T(8,128)(2,1)}, bf16[4,4,128,128]{3,2,1,0:T(8,128)(2,1)S(1)}, u32[]{:S(2)}, u32[]{:S(2)}) %collective-permute-start) | collective-permute-done | bytes 524320 | tf_op jit(solution)/shard_map/while/body/eval_jaxpr/ppermute | solution.py:16
  160.8 48.6 %while.50 = (s32[]{:T(128)}, f32[4,4,128,128]{3,2,1,0:T(8,128)S(1)}, s32[4,4]{1,0:T(4,128)S(1)}, bf16[768,32,128]{2,0,1:T(8,128)(2,1)}, s32[4]{0:T(128)S(1)}, /*...) while((s32[]{:T(128)}, f32[4,4,128,128]{3,2,1,0:T(8,128)S(1)}, ...), condition=%wide.region_3.3_spmd, body=%wide.region_1.2_spmd.sunk | while | flops 204244144 | bytes 3768029 | solution.py:38
  167.0 3.9 compare_reduce_fusion.2
  179.2 3.9 compare_reduce_fusion.2
  191.3 3.9 compare_reduce_fusion.2
  203.5 3.9 compare_reduce_fusion.2
  211.8 26.6 %collective-permute-done = bf16[4,4,128,128]{3,2,1,0:T(8,128)(2,1)S(1)} collective-permute-done((bf16[4,4,128,128]{3,2,1,0:T(8,128)(2,1)}, bf16[4,4,128,128]{3,2,1,0:T(8,128)(2,1)S(1)}, u32[]{:S(2)}, u32[]{:S(2)}) %collective-permute-start) | collective-permute-done | bytes 524320 | tf_op jit(solution)/shard_map/while/body/eval_jaxpr/ppermute | solution.py:16
  239.4 48.6 %while.50 = (s32[]{:T(128)}, f32[4,4,128,128]{3,2,1,0:T(8,128)S(1)}, s32[4,4]{1,0:T(4,128)S(1)}, bf16[768,32,128]{2,0,1:T(8,128)(2,1)}, s32[4]{0:T(128)S(1)}, /*...) while((s32[]{:T(128)}, f32[4,4,128,128]{3,2,1,0:T(8,128)S(1)}, ...), condition=%wide.region_3.3_spmd, body=%wide.region_1.2_spmd.sunk | while | flops 204244144 | bytes 3768029 | solution.py:38
  282.1 3.9 compare_reduce_fusion.2
  289.5 26.6 %collective-permute-done = bf16[4,4,128,128]{3,2,1,0:T(8,128)(2,1)S(1)} collective-permute-done((bf16[4,4,128,128]{3,2,1,0:T(8,128)(2,1)}, bf16[4,4,128,128]{3,2,1,0:T(8,128)(2,1)S(1)}, u32[]{:S(2)}, u32[]{:S(2)}) %collective-permute-start) | collective-permute-done | bytes 524320 | tf_op jit(solution)/shard_map/while/body/eval_jaxpr/ppermute | solution.py:16
  317.1 48.6 %while.50 = (s32[]{:T(128)}, f32[4,4,128,128]{3,2,1,0:T(8,128)S(1)}, s32[4,4]{1,0:T(4,128)S(1)}, bf16[768,32,128]{2,0,1:T(8,128)(2,1)}, s32[4]{0:T(128)S(1)}, /*...) while((s32[]{:T(128)}, f32[4,4,128,128]{3,2,1,0:T(8,128)S(1)}, ...), condition=%wide.region_3.3_spmd, body=%wide.region_1.2_spmd.sunk | while | flops 204244144 | bytes 3768029 | solution.py:38
  323.3 3.9 compare_reduce_fusion.2
  335.5 3.9 compare_reduce_fusion.2
  366.7 26.2 %collective-permute-done = bf16[4,4,128,128]{3,2,1,0:T(8,128)(2,1)S(1)} collective-permute-done((bf16[4,4,128,128]{3,2,1,0:T(8,128)(2,1)}, bf16[4,4,128,128]{3,2,1,0:T(8,128)(2,1)S(1)}, u32[]{:S(2)}, u32[]{:S(2)}) %collective-permute-start) | collective-permute-done | bytes 524320 | tf_op jit(solution)/shard_map/while/body/eval_jaxpr/ppermute | solution.py:16
  393.8 48.6 %while.50 = (s32[]{:T(128)}, f32[4,4,128,128]{3,2,1,0:T(8,128)S(1)}, s32[4,4]{1,0:T(4,128)S(1)}, bf16[768,32,128]{2,0,1:T(8,128)(2,1)}, s32[4]{0:T(128)S(1)}, /*...) while((s32[]{:T(128)}, f32[4,4,128,128]{3,2,1,0:T(8,128)S(1)}, ...), condition=%wide.region_3.3_spmd, body=%wide.region_1.2_spmd.sunk | while | flops 204244144 | bytes 3768029 | solution.py:38
  443.5 25.3 %collective-permute-done = bf16[4,4,128,128]{3,2,1,0:T(8,128)(2,1)S(1)} collective-permute-done((bf16[4,4,128,128]{3,2,1,0:T(8,128)(2,1)}, bf16[4,4,128,128]{3,2,1,0:T(8,128)(2,1)S(1)}, u32[]{:S(2)}, u32[]{:S(2)}) %collective-permute-start) | collective-permute-done | bytes 524320 | tf_op jit(solution)/shard_map/while/body/eval_jaxpr/ppermute | solution.py:16
  469.7 48.6 %while.50 = (s32[]{:T(128)}, f32[4,4,128,128]{3,2,1,0:T(8,128)S(1)}, s32[4,4]{1,0:T(4,128)S(1)}, bf16[768,32,128]{2,0,1:T(8,128)(2,1)}, s32[4]{0:T(128)S(1)}, /*...) while((s32[]{:T(128)}, f32[4,4,128,128]{3,2,1,0:T(8,128)S(1)}, ...), condition=%wide.region_3.3_spmd, body=%wide.region_1.2_spmd.sunk | while | flops 204244144 | bytes 3768029 | solution.py:38
  519.4 24.4 %collective-permute-done = bf16[4,4,128,128]{3,2,1,0:T(8,128)(2,1)S(1)} collective-permute-done((bf16[4,4,128,128]{3,2,1,0:T(8,128)(2,1)}, bf16[4,4,128,128]{3,2,1,0:T(8,128)(2,1)S(1)}, u32[]{:S(2)}, u32[]{:S(2)}) %collective-permute-start) | collective-permute-done | bytes 524320 | tf_op jit(solution)/shard_map/while/body/eval_jaxpr/ppermute | solution.py:16
  544.6 48.6 %while.50 = (s32[]{:T(128)}, f32[4,4,128,128]{3,2,1,0:T(8,128)S(1)}, s32[4,4]{1,0:T(4,128)S(1)}, bf16[768,32,128]{2,0,1:T(8,128)(2,1)}, s32[4]{0:T(128)S(1)}, /*...) while((s32[]{:T(128)}, f32[4,4,128,128]{3,2,1,0:T(8,128)S(1)}, ...), condition=%wide.region_3.3_spmd, body=%wide.region_1.2_spmd.sunk | while | flops 204244144 | bytes 3768029 | solution.py:38
  594.3 24.2 %collective-permute-done = bf16[4,4,128,128]{3,2,1,0:T(8,128)(2,1)S(1)} collective-permute-done((bf16[4,4,128,128]{3,2,1,0:T(8,128)(2,1)}, bf16[4,4,128,128]{3,2,1,0:T(8,128)(2,1)S(1)}, u32[]{:S(2)}, u32[]{:S(2)}) %collective-permute-start) | collective-permute-done | bytes 524320 | tf_op jit(solution)/shard_map/while/body/eval_jaxpr/ppermute | solution.py:16
  619.4 48.6 %while.50 = (s32[]{:T(128)}, f32[4,4,128,128]{3,2,1,0:T(8,128)S(1)}, s32[4,4]{1,0:T(4,128)S(1)}, bf16[768,32,128]{2,0,1:T(8,128)(2,1)}, s32[4]{0:T(128)S(1)}, /*...) while((s32[]{:T(128)}, f32[4,4,128,128]{3,2,1,0:T(8,128)S(1)}, ...), condition=%wide.region_3.3_spmd, body=%wide.region_1.2_spmd.sunk | while | flops 204244144 | bytes 3768029 | solution.py:38
  669.1 24.2 %collective-permute-done = bf16[4,4,128,128]{3,2,1,0:T(8,128)(2,1)S(1)} collective-permute-done((bf16[4,4,128,128]{3,2,1,0:T(8,128)(2,1)}, bf16[4,4,128,128]{3,2,1,0:T(8,128)(2,1)S(1)}, u32[]{:S(2)}, u32[]{:S(2)}) %collective-permute-start) | collective-permute-done | bytes 524320 | tf_op jit(solution)/shard_map/while/body/eval_jaxpr/ppermute | solution.py:16
  694.2 48.6 %while.50 = (s32[]{:T(128)}, f32[4,4,128,128]{3,2,1,0:T(8,128)S(1)}, s32[4,4]{1,0:T(4,128)S(1)}, bf16[768,32,128]{2,0,1:T(8,128)(2,1)}, s32[4]{0:T(128)S(1)}, /*...) while((s32[]{:T(128)}, f32[4,4,128,128]{3,2,1,0:T(8,128)S(1)}, ...), condition=%wide.region_3.3_spmd, body=%wide.region_1.2_spmd.sunk | while | flops 204244144 | bytes 3768029 | solution.py:38
  743.9 24.2 %collective-permute-done = bf16[4,4,128,128]{3,2,1,0:T(8,128)(2,1)S(1)} collective-permute-done((bf16[4,4,128,128]{3,2,1,0:T(8,128)(2,1)}, bf16[4,4,128,128]{3,2,1,0:T(8,128)(2,1)S(1)}, u32[]{:S(2)}, u32[]{:S(2)}) %collective-permute-start) | collective-permute-done | bytes 524320 | tf_op jit(solution)/shard_map/while/body/eval_jaxpr/ppermute | solution.py:16
  769.0 48.6 %while.50 = (s32[]{:T(128)}, f32[4,4,128,128]{3,2,1,0:T(8,128)S(1)}, s32[4,4]{1,0:T(4,128)S(1)}, bf16[768,32,128]{2,0,1:T(8,128)(2,1)}, s32[4]{0:T(128)S(1)}, /*...) while((s32[]{:T(128)}, f32[4,4,128,128]{3,2,1,0:T(8,128)S(1)}, ...), condition=%wide.region_3.3_spmd, body=%wide.region_1.2_spmd.sunk | while | flops 204244144 | bytes 3768029 | solution.py:38
  818.7 24.2 %collective-permute-done = bf16[4,4,128,128]{3,2,1,0:T(8,128)(2,1)S(1)} collective-permute-done((bf16[4,4,128,128]{3,2,1,0:T(8,128)(2,1)}, bf16[4,4,128,128]{3,2,1,0:T(8,128)(2,1)S(1)}, u32[]{:S(2)}, u32[]{:S(2)}) %collective-permute-start) | collective-permute-done | bytes 524320 | tf_op jit(solution)/shard_map/while/body/eval_jaxpr/ppermute | solution.py:16
  843.9 48.6 %while.50 = (s32[]{:T(128)}, f32[4,4,128,128]{3,2,1,0:T(8,128)S(1)}, s32[4,4]{1,0:T(4,128)S(1)}, bf16[768,32,128]{2,0,1:T(8,128)(2,1)}, s32[4]{0:T(128)S(1)}, /*...) while((s32[]{:T(128)}, f32[4,4,128,128]{3,2,1,0:T(8,128)S(1)}, ...), condition=%wide.region_3.3_spmd, body=%wide.region_1.2_spmd.sunk | while | flops 204244144 | bytes 3768029 | solution.py:38
  893.5 24.2 %collective-permute-done = bf16[4,4,128,128]{3,2,1,0:T(8,128)(2,1)S(1)} collective-permute-done((bf16[4,4,128,128]{3,2,1,0:T(8,128)(2,1)}, bf16[4,4,128,128]{3,2,1,0:T(8,128)(2,1)S(1)}, u32[]{:S(2)}, u32[]{:S(2)}) %collective-permute-start) | collective-permute-done | bytes 524320 | tf_op jit(solution)/shard_map/while/body/eval_jaxpr/ppermute | solution.py:16
  918.7 48.6 %while.50 = (s32[]{:T(128)}, f32[4,4,128,128]{3,2,1,0:T(8,128)S(1)}, s32[4,4]{1,0:T(4,128)S(1)}, bf16[768,32,128]{2,0,1:T(8,128)(2,1)}, s32[4]{0:T(128)S(1)}, /*...) while((s32[]{:T(128)}, f32[4,4,128,128]{3,2,1,0:T(8,128)S(1)}, ...), condition=%wide.region_3.3_spmd, body=%wide.region_1.2_spmd.sunk | while | flops 204244144 | bytes 3768029 | solution.py:38
  968.4 24.2 %collective-permute-done = bf16[4,4,128,128]{3,2,1,0:T(8,128)(2,1)S(1)} collective-permute-done((bf16[4,4,128,128]{3,2,1,0:T(8,128)(2,1)}, bf16[4,4,128,128]{3,2,1,0:T(8,128)(2,1)S(1)}, u32[]{:S(2)}, u32[]{:S(2)}) %collective-permute-start) | collective-permute-done | bytes 524320 | tf_op jit(solution)/shard_map/while/body/eval_jaxpr/ppermute | solution.py:16
  993.5 48.6 %while.50 = (s32[]{:T(128)}, f32[4,4,128,128]{3,2,1,0:T(8,128)S(1)}, s32[4,4]{1,0:T(4,128)S(1)}, bf16[768,32,128]{2,0,1:T(8,128)(2,1)}, s32[4]{0:T(128)S(1)}, /*...) while((s32[]{:T(128)}, f32[4,4,128,128]{3,2,1,0:T(8,128)S(1)}, ...), condition=%wide.region_3.3_spmd, body=%wide.region_1.2_spmd.sunk | while | flops 204244144 | bytes 3768029 | solution.py:38
  1043.2 24.2 %collective-permute-done = bf16[4,4,128,128]{3,2,1,0:T(8,128)(2,1)S(1)} collective-permute-done((bf16[4,4,128,128]{3,2,1,0:T(8,128)(2,1)}, bf16[4,4,128,128]{3,2,1,0:T(8,128)(2,1)S(1)}, u32[]{:S(2)}, u32[]{:S(2)}) %collective-permute-start) | collective-permute-done | bytes 524320 | tf_op jit(solution)/shard_map/while/body/eval_jaxpr/ppermute | solution.py:16
  1068.3 48.6 %while.50 = (s32[]{:T(128)}, f32[4,4,128,128]{3,2,1,0:T(8,128)S(1)}, s32[4,4]{1,0:T(4,128)S(1)}, bf16[768,32,128]{2,0,1:T(8,128)(2,1)}, s32[4]{0:T(128)S(1)}, /*...) while((s32[]{:T(128)}, f32[4,4,128,128]{3,2,1,0:T(8,128)S(1)}, ...), condition=%wide.region_3.3_spmd, body=%wide.region_1.2_spmd.sunk | while | flops 204244144 | bytes 3768029 | solution.py:38
  1118.0 24.2 %collective-permute-done = bf16[4,4,128,128]{3,2,1,0:T(8,128)(2,1)S(1)} collective-permute-done((bf16[4,4,128,128]{3,2,1,0:T(8,128)(2,1)}, bf16[4,4,128,128]{3,2,1,0:T(8,128)(2,1)S(1)}, u32[]{:S(2)}, u32[]{:S(2)}) %collective-permute-start) | collective-permute-done | bytes 524320 | tf_op jit(solution)/shard_map/while/body/eval_jaxpr/ppermute | solution.py:16
  1143.1 48.6 %while.50 = (s32[]{:T(128)}, f32[4,4,128,128]{3,2,1,0:T(8,128)S(1)}, s32[4,4]{1,0:T(4,128)S(1)}, bf16[768,32,128]{2,0,1:T(8,128)(2,1)}, s32[4]{0:T(128)S(1)}, /*...) while((s32[]{:T(128)}, f32[4,4,128,128]{3,2,1,0:T(8,128)S(1)}, ...), condition=%wide.region_3.3_spmd, body=%wide.region_1.2_spmd.sunk | while | flops 204244144 | bytes 3768029 | solution.py:38
  1192.8 24.2 %collective-permute-done = bf16[4,4,128,128]{3,2,1,0:T(8,128)(2,1)S(1)} collective-permute-done((bf16[4,4,128,128]{3,2,1,0:T(8,128)(2,1)}, bf16[4,4,128,128]{3,2,1,0:T(8,128)(2,1)S(1)}, u32[]{:S(2)}, u32[]{:S(2)}) %collective-permute-start) | collective-permute-done | bytes 524320 | tf_op jit(solution)/shard_map/while/body/eval_jaxpr/ppermute | solution.py:16
  1217.9 48.6 %while.50 = (s32[]{:T(128)}, f32[4,4,128,128]{3,2,1,0:T(8,128)S(1)}, s32[4,4]{1,0:T(4,128)S(1)}, bf16[768,32,128]{2,0,1:T(8,128)(2,1)}, s32[4]{0:T(128)S(1)}, /*...) while((s32[]{:T(128)}, f32[4,4,128,128]{3,2,1,0:T(8,128)S(1)}, ...), condition=%wide.region_3.3_spmd, body=%wide.region_1.2_spmd.sunk | while | flops 204244144 | bytes 3768029 | solution.py:38
  1267.6 24.2 %collective-permute-done = bf16[4,4,128,128]{3,2,1,0:T(8,128)(2,1)S(1)} collective-permute-done((bf16[4,4,128,128]{3,2,1,0:T(8,128)(2,1)}, bf16[4,4,128,128]{3,2,1,0:T(8,128)(2,1)S(1)}, u32[]{:S(2)}, u32[]{:S(2)}) %collective-permute-start) | collective-permute-done | bytes 524320 | tf_op jit(solution)/shard_map/while/body/eval_jaxpr/ppermute | solution.py:16
  1291.9 4.5 fusion.34
  (725 shorter events, 772.3 us)
Async XLA Ops:
  32.3 8.7 copy-start
  32.3 8.8 copy-start.1
  32.3 9.0 copy-start.2
  80.3 1211.6 %copy-start.3 = (s32[4]{0:T(128)S(1)}, s32[4]{0:T(128)}, u32[]{:S(2)}) copy-start(s32[4]{0:T(128)} %param.14) | copy-start | bytes 52
  130.9 29.0 %collective-permute-start.1 = (f32[4,4,128,128]{3,2,1,0:T(8,128)}, f32[4,4,128,128]{3,2,1,0:T(8,128)S(1)}, u32[]{:S(2)}, u32[]{:S(2)}) collective-permute-start(f32[4,4,128,128]{3,2,1,0:T(8,128)} %add.197), channel_id=1, source_target_pairs={{0,16},{16,32},{32,48},{48,64},{64,80},{80,96},{96,112},{112,128},... | collective-permute-start | bytes 3145736 | tf_op jit(solution)/shard_map/while/body/eval_jaxpr/ppermute | solution.py:16
  131.2 28.6 %collective-permute-start = (bf16[4,4,128,128]{3,2,1,0:T(8,128)(2,1)}, bf16[4,4,128,128]{3,2,1,0:T(8,128)(2,1)S(1)}, u32[]{:S(2)}, u32[]{:S(2)}) collective-permute-start(bf16[4,4,128,128]{3,2,1,0:T(8,128)(2,1)} %get-tuple-element.539), channel_id=1, source_target_pairs={{0,16},{16,32},{32,48},{48,64},{64,80},{80,96},{96,112},{112,128},... | collective-permute-start | bytes 1572872 | tf_op jit(solution)/shard_map/while/body/eval_jaxpr/ppermute | solution.py:16
  210.4 28.0 %collective-permute-start.1 = (f32[4,4,128,128]{3,2,1,0:T(8,128)}, f32[4,4,128,128]{3,2,1,0:T(8,128)S(1)}, u32[]{:S(2)}, u32[]{:S(2)}) collective-permute-start(f32[4,4,128,128]{3,2,1,0:T(8,128)} %add.197), channel_id=1, source_target_pairs={{0,16},{16,32},{32,48},{48,64},{64,80},{80,96},{96,112},{112,128},... | collective-permute-start | bytes 3145736 | tf_op jit(solution)/shard_map/while/body/eval_jaxpr/ppermute | solution.py:16
  210.4 28.0 %collective-permute-start = (bf16[4,4,128,128]{3,2,1,0:T(8,128)(2,1)}, bf16[4,4,128,128]{3,2,1,0:T(8,128)(2,1)S(1)}, u32[]{:S(2)}, u32[]{:S(2)}) collective-permute-start(bf16[4,4,128,128]{3,2,1,0:T(8,128)(2,1)} %get-tuple-element.539), channel_id=1, source_target_pairs={{0,16},{16,32},{32,48},{48,64},{64,80},{80,96},{96,112},{112,128},... | collective-permute-start | bytes 1572872 | tf_op jit(solution)/shard_map/while/body/eval_jaxpr/ppermute | solution.py:16
  289.0 27.1 %collective-permute-start.1 = (f32[4,4,128,128]{3,2,1,0:T(8,128)}, f32[4,4,128,128]{3,2,1,0:T(8,128)S(1)}, u32[]{:S(2)}, u32[]{:S(2)}) collective-permute-start(f32[4,4,128,128]{3,2,1,0:T(8,128)} %add.197), channel_id=1, source_target_pairs={{0,16},{16,32},{32,48},{48,64},{64,80},{80,96},{96,112},{112,128},... | collective-permute-start | bytes 3145736 | tf_op jit(solution)/shard_map/while/body/eval_jaxpr/ppermute | solution.py:16
  289.1 27.1 %collective-permute-start = (bf16[4,4,128,128]{3,2,1,0:T(8,128)(2,1)}, bf16[4,4,128,128]{3,2,1,0:T(8,128)(2,1)S(1)}, u32[]{:S(2)}, u32[]{:S(2)}) collective-permute-start(bf16[4,4,128,128]{3,2,1,0:T(8,128)(2,1)} %get-tuple-element.539), channel_id=1, source_target_pairs={{0,16},{16,32},{32,48},{48,64},{64,80},{80,96},{96,112},{112,128},... | collective-permute-start | bytes 1572872 | tf_op jit(solution)/shard_map/while/body/eval_jaxpr/ppermute | solution.py:16
  366.7 26.2 %collective-permute-start.1 = (f32[4,4,128,128]{3,2,1,0:T(8,128)}, f32[4,4,128,128]{3,2,1,0:T(8,128)S(1)}, u32[]{:S(2)}, u32[]{:S(2)}) collective-permute-start(f32[4,4,128,128]{3,2,1,0:T(8,128)} %add.197), channel_id=1, source_target_pairs={{0,16},{16,32},{32,48},{48,64},{64,80},{80,96},{96,112},{112,128},... | collective-permute-start | bytes 3145736 | tf_op jit(solution)/shard_map/while/body/eval_jaxpr/ppermute | solution.py:16
  366.7 26.2 %collective-permute-start = (bf16[4,4,128,128]{3,2,1,0:T(8,128)(2,1)}, bf16[4,4,128,128]{3,2,1,0:T(8,128)(2,1)S(1)}, u32[]{:S(2)}, u32[]{:S(2)}) collective-permute-start(bf16[4,4,128,128]{3,2,1,0:T(8,128)(2,1)} %get-tuple-element.539), channel_id=1, source_target_pairs={{0,16},{16,32},{32,48},{48,64},{64,80},{80,96},{96,112},{112,128},... | collective-permute-start | bytes 1572872 | tf_op jit(solution)/shard_map/while/body/eval_jaxpr/ppermute | solution.py:16
  443.5 25.3 %collective-permute-start.1 = (f32[4,4,128,128]{3,2,1,0:T(8,128)}, f32[4,4,128,128]{3,2,1,0:T(8,128)S(1)}, u32[]{:S(2)}, u32[]{:S(2)}) collective-permute-start(f32[4,4,128,128]{3,2,1,0:T(8,128)} %add.197), channel_id=1, source_target_pairs={{0,16},{16,32},{32,48},{48,64},{64,80},{80,96},{96,112},{112,128},... | collective-permute-start | bytes 3145736 | tf_op jit(solution)/shard_map/while/body/eval_jaxpr/ppermute | solution.py:16
  443.5 25.3 %collective-permute-start = (bf16[4,4,128,128]{3,2,1,0:T(8,128)(2,1)}, bf16[4,4,128,128]{3,2,1,0:T(8,128)(2,1)S(1)}, u32[]{:S(2)}, u32[]{:S(2)}) collective-permute-start(bf16[4,4,128,128]{3,2,1,0:T(8,128)(2,1)} %get-tuple-element.539), channel_id=1, source_target_pairs={{0,16},{16,32},{32,48},{48,64},{64,80},{80,96},{96,112},{112,128},... | collective-permute-start | bytes 1572872 | tf_op jit(solution)/shard_map/while/body/eval_jaxpr/ppermute | solution.py:16
  519.4 24.4 %collective-permute-start.1 = (f32[4,4,128,128]{3,2,1,0:T(8,128)}, f32[4,4,128,128]{3,2,1,0:T(8,128)S(1)}, u32[]{:S(2)}, u32[]{:S(2)}) collective-permute-start(f32[4,4,128,128]{3,2,1,0:T(8,128)} %add.197), channel_id=1, source_target_pairs={{0,16},{16,32},{32,48},{48,64},{64,80},{80,96},{96,112},{112,128},... | collective-permute-start | bytes 3145736 | tf_op jit(solution)/shard_map/while/body/eval_jaxpr/ppermute | solution.py:16
  519.4 24.4 %collective-permute-start = (bf16[4,4,128,128]{3,2,1,0:T(8,128)(2,1)}, bf16[4,4,128,128]{3,2,1,0:T(8,128)(2,1)S(1)}, u32[]{:S(2)}, u32[]{:S(2)}) collective-permute-start(bf16[4,4,128,128]{3,2,1,0:T(8,128)(2,1)} %get-tuple-element.539), channel_id=1, source_target_pairs={{0,16},{16,32},{32,48},{48,64},{64,80},{80,96},{96,112},{112,128},... | collective-permute-start | bytes 1572872 | tf_op jit(solution)/shard_map/while/body/eval_jaxpr/ppermute | solution.py:16
  594.3 24.2 %collective-permute-start.1 = (f32[4,4,128,128]{3,2,1,0:T(8,128)}, f32[4,4,128,128]{3,2,1,0:T(8,128)S(1)}, u32[]{:S(2)}, u32[]{:S(2)}) collective-permute-start(f32[4,4,128,128]{3,2,1,0:T(8,128)} %add.197), channel_id=1, source_target_pairs={{0,16},{16,32},{32,48},{48,64},{64,80},{80,96},{96,112},{112,128},... | collective-permute-start | bytes 3145736 | tf_op jit(solution)/shard_map/while/body/eval_jaxpr/ppermute | solution.py:16
  594.3 24.2 %collective-permute-start = (bf16[4,4,128,128]{3,2,1,0:T(8,128)(2,1)}, bf16[4,4,128,128]{3,2,1,0:T(8,128)(2,1)S(1)}, u32[]{:S(2)}, u32[]{:S(2)}) collective-permute-start(bf16[4,4,128,128]{3,2,1,0:T(8,128)(2,1)} %get-tuple-element.539), channel_id=1, source_target_pairs={{0,16},{16,32},{32,48},{48,64},{64,80},{80,96},{96,112},{112,128},... | collective-permute-start | bytes 1572872 | tf_op jit(solution)/shard_map/while/body/eval_jaxpr/ppermute | solution.py:16
  669.1 24.2 %collective-permute-start.1 = (f32[4,4,128,128]{3,2,1,0:T(8,128)}, f32[4,4,128,128]{3,2,1,0:T(8,128)S(1)}, u32[]{:S(2)}, u32[]{:S(2)}) collective-permute-start(f32[4,4,128,128]{3,2,1,0:T(8,128)} %add.197), channel_id=1, source_target_pairs={{0,16},{16,32},{32,48},{48,64},{64,80},{80,96},{96,112},{112,128},... | collective-permute-start | bytes 3145736 | tf_op jit(solution)/shard_map/while/body/eval_jaxpr/ppermute | solution.py:16
  669.1 24.2 %collective-permute-start = (bf16[4,4,128,128]{3,2,1,0:T(8,128)(2,1)}, bf16[4,4,128,128]{3,2,1,0:T(8,128)(2,1)S(1)}, u32[]{:S(2)}, u32[]{:S(2)}) collective-permute-start(bf16[4,4,128,128]{3,2,1,0:T(8,128)(2,1)} %get-tuple-element.539), channel_id=1, source_target_pairs={{0,16},{16,32},{32,48},{48,64},{64,80},{80,96},{96,112},{112,128},... | collective-permute-start | bytes 1572872 | tf_op jit(solution)/shard_map/while/body/eval_jaxpr/ppermute | solution.py:16
  743.9 24.2 %collective-permute-start.1 = (f32[4,4,128,128]{3,2,1,0:T(8,128)}, f32[4,4,128,128]{3,2,1,0:T(8,128)S(1)}, u32[]{:S(2)}, u32[]{:S(2)}) collective-permute-start(f32[4,4,128,128]{3,2,1,0:T(8,128)} %add.197), channel_id=1, source_target_pairs={{0,16},{16,32},{32,48},{48,64},{64,80},{80,96},{96,112},{112,128},... | collective-permute-start | bytes 3145736 | tf_op jit(solution)/shard_map/while/body/eval_jaxpr/ppermute | solution.py:16
  743.9 24.2 %collective-permute-start = (bf16[4,4,128,128]{3,2,1,0:T(8,128)(2,1)}, bf16[4,4,128,128]{3,2,1,0:T(8,128)(2,1)S(1)}, u32[]{:S(2)}, u32[]{:S(2)}) collective-permute-start(bf16[4,4,128,128]{3,2,1,0:T(8,128)(2,1)} %get-tuple-element.539), channel_id=1, source_target_pairs={{0,16},{16,32},{32,48},{48,64},{64,80},{80,96},{96,112},{112,128},... | collective-permute-start | bytes 1572872 | tf_op jit(solution)/shard_map/while/body/eval_jaxpr/ppermute | solution.py:16
  818.7 24.2 %collective-permute-start.1 = (f32[4,4,128,128]{3,2,1,0:T(8,128)}, f32[4,4,128,128]{3,2,1,0:T(8,128)S(1)}, u32[]{:S(2)}, u32[]{:S(2)}) collective-permute-start(f32[4,4,128,128]{3,2,1,0:T(8,128)} %add.197), channel_id=1, source_target_pairs={{0,16},{16,32},{32,48},{48,64},{64,80},{80,96},{96,112},{112,128},... | collective-permute-start | bytes 3145736 | tf_op jit(solution)/shard_map/while/body/eval_jaxpr/ppermute | solution.py:16
  818.7 24.2 %collective-permute-start = (bf16[4,4,128,128]{3,2,1,0:T(8,128)(2,1)}, bf16[4,4,128,128]{3,2,1,0:T(8,128)(2,1)S(1)}, u32[]{:S(2)}, u32[]{:S(2)}) collective-permute-start(bf16[4,4,128,128]{3,2,1,0:T(8,128)(2,1)} %get-tuple-element.539), channel_id=1, source_target_pairs={{0,16},{16,32},{32,48},{48,64},{64,80},{80,96},{96,112},{112,128},... | collective-permute-start | bytes 1572872 | tf_op jit(solution)/shard_map/while/body/eval_jaxpr/ppermute | solution.py:16
  893.5 24.2 %collective-permute-start.1 = (f32[4,4,128,128]{3,2,1,0:T(8,128)}, f32[4,4,128,128]{3,2,1,0:T(8,128)S(1)}, u32[]{:S(2)}, u32[]{:S(2)}) collective-permute-start(f32[4,4,128,128]{3,2,1,0:T(8,128)} %add.197), channel_id=1, source_target_pairs={{0,16},{16,32},{32,48},{48,64},{64,80},{80,96},{96,112},{112,128},... | collective-permute-start | bytes 3145736 | tf_op jit(solution)/shard_map/while/body/eval_jaxpr/ppermute | solution.py:16
  893.5 24.2 %collective-permute-start = (bf16[4,4,128,128]{3,2,1,0:T(8,128)(2,1)}, bf16[4,4,128,128]{3,2,1,0:T(8,128)(2,1)S(1)}, u32[]{:S(2)}, u32[]{:S(2)}) collective-permute-start(bf16[4,4,128,128]{3,2,1,0:T(8,128)(2,1)} %get-tuple-element.539), channel_id=1, source_target_pairs={{0,16},{16,32},{32,48},{48,64},{64,80},{80,96},{96,112},{112,128},... | collective-permute-start | bytes 1572872 | tf_op jit(solution)/shard_map/while/body/eval_jaxpr/ppermute | solution.py:16
  968.4 24.2 %collective-permute-start.1 = (f32[4,4,128,128]{3,2,1,0:T(8,128)}, f32[4,4,128,128]{3,2,1,0:T(8,128)S(1)}, u32[]{:S(2)}, u32[]{:S(2)}) collective-permute-start(f32[4,4,128,128]{3,2,1,0:T(8,128)} %add.197), channel_id=1, source_target_pairs={{0,16},{16,32},{32,48},{48,64},{64,80},{80,96},{96,112},{112,128},... | collective-permute-start | bytes 3145736 | tf_op jit(solution)/shard_map/while/body/eval_jaxpr/ppermute | solution.py:16
  968.4 24.2 %collective-permute-start = (bf16[4,4,128,128]{3,2,1,0:T(8,128)(2,1)}, bf16[4,4,128,128]{3,2,1,0:T(8,128)(2,1)S(1)}, u32[]{:S(2)}, u32[]{:S(2)}) collective-permute-start(bf16[4,4,128,128]{3,2,1,0:T(8,128)(2,1)} %get-tuple-element.539), channel_id=1, source_target_pairs={{0,16},{16,32},{32,48},{48,64},{64,80},{80,96},{96,112},{112,128},... | collective-permute-start | bytes 1572872 | tf_op jit(solution)/shard_map/while/body/eval_jaxpr/ppermute | solution.py:16
  1043.2 24.2 %collective-permute-start.1 = (f32[4,4,128,128]{3,2,1,0:T(8,128)}, f32[4,4,128,128]{3,2,1,0:T(8,128)S(1)}, u32[]{:S(2)}, u32[]{:S(2)}) collective-permute-start(f32[4,4,128,128]{3,2,1,0:T(8,128)} %add.197), channel_id=1, source_target_pairs={{0,16},{16,32},{32,48},{48,64},{64,80},{80,96},{96,112},{112,128},... | collective-permute-start | bytes 3145736 | tf_op jit(solution)/shard_map/while/body/eval_jaxpr/ppermute | solution.py:16
  1043.2 24.2 %collective-permute-start = (bf16[4,4,128,128]{3,2,1,0:T(8,128)(2,1)}, bf16[4,4,128,128]{3,2,1,0:T(8,128)(2,1)S(1)}, u32[]{:S(2)}, u32[]{:S(2)}) collective-permute-start(bf16[4,4,128,128]{3,2,1,0:T(8,128)(2,1)} %get-tuple-element.539), channel_id=1, source_target_pairs={{0,16},{16,32},{32,48},{48,64},{64,80},{80,96},{96,112},{112,128},... | collective-permute-start | bytes 1572872 | tf_op jit(solution)/shard_map/while/body/eval_jaxpr/ppermute | solution.py:16
  1118.0 24.2 %collective-permute-start.1 = (f32[4,4,128,128]{3,2,1,0:T(8,128)}, f32[4,4,128,128]{3,2,1,0:T(8,128)S(1)}, u32[]{:S(2)}, u32[]{:S(2)}) collective-permute-start(f32[4,4,128,128]{3,2,1,0:T(8,128)} %add.197), channel_id=1, source_target_pairs={{0,16},{16,32},{32,48},{48,64},{64,80},{80,96},{96,112},{112,128},... | collective-permute-start | bytes 3145736 | tf_op jit(solution)/shard_map/while/body/eval_jaxpr/ppermute | solution.py:16
  1118.0 24.2 %collective-permute-start = (bf16[4,4,128,128]{3,2,1,0:T(8,128)(2,1)}, bf16[4,4,128,128]{3,2,1,0:T(8,128)(2,1)S(1)}, u32[]{:S(2)}, u32[]{:S(2)}) collective-permute-start(bf16[4,4,128,128]{3,2,1,0:T(8,128)(2,1)} %get-tuple-element.539), channel_id=1, source_target_pairs={{0,16},{16,32},{32,48},{48,64},{64,80},{80,96},{96,112},{112,128},... | collective-permute-start | bytes 1572872 | tf_op jit(solution)/shard_map/while/body/eval_jaxpr/ppermute | solution.py:16
  1192.8 24.2 %collective-permute-start.1 = (f32[4,4,128,128]{3,2,1,0:T(8,128)}, f32[4,4,128,128]{3,2,1,0:T(8,128)S(1)}, u32[]{:S(2)}, u32[]{:S(2)}) collective-permute-start(f32[4,4,128,128]{3,2,1,0:T(8,128)} %add.197), channel_id=1, source_target_pairs={{0,16},{16,32},{32,48},{48,64},{64,80},{80,96},{96,112},{112,128},... | collective-permute-start | bytes 3145736 | tf_op jit(solution)/shard_map/while/body/eval_jaxpr/ppermute | solution.py:16
  1192.8 24.2 %collective-permute-start = (bf16[4,4,128,128]{3,2,1,0:T(8,128)(2,1)}, bf16[4,4,128,128]{3,2,1,0:T(8,128)(2,1)S(1)}, u32[]{:S(2)}, u32[]{:S(2)}) collective-permute-start(bf16[4,4,128,128]{3,2,1,0:T(8,128)(2,1)} %get-tuple-element.539), channel_id=1, source_target_pairs={{0,16},{16,32},{32,48},{48,64},{64,80},{80,96},{96,112},{112,128},... | collective-permute-start | bytes 1572872 | tf_op jit(solution)/shard_map/while/body/eval_jaxpr/ppermute | solution.py:16
  1267.6 24.2 %collective-permute-start.1 = (f32[4,4,128,128]{3,2,1,0:T(8,128)}, f32[4,4,128,128]{3,2,1,0:T(8,128)S(1)}, u32[]{:S(2)}, u32[]{:S(2)}) collective-permute-start(f32[4,4,128,128]{3,2,1,0:T(8,128)} %add.197), channel_id=1, source_target_pairs={{0,16},{16,32},{32,48},{48,64},{64,80},{80,96},{96,112},{112,128},... | collective-permute-start | bytes 3145736 | tf_op jit(solution)/shard_map/while/body/eval_jaxpr/ppermute | solution.py:16
  1267.6 24.2 %collective-permute-start = (bf16[4,4,128,128]{3,2,1,0:T(8,128)(2,1)}, bf16[4,4,128,128]{3,2,1,0:T(8,128)(2,1)S(1)}, u32[]{:S(2)}, u32[]{:S(2)}) collective-permute-start(bf16[4,4,128,128]{3,2,1,0:T(8,128)(2,1)} %get-tuple-element.539), channel_id=1, source_target_pairs={{0,16},{16,32},{32,48},{48,64},{64,80},{80,96},{96,112},{112,128},... | collective-permute-start | bytes 1572872 | tf_op jit(solution)/shard_map/while/body/eval_jaxpr/ppermute | solution.py:16
where the time goes:
time: 1300 us
  waiting for transfers between devices  398 us (31%)
  other arithmetic  364 us (28%)
  local copies, waits for them, and re-layouts  342 us (26%)
  matrix products  123 us (9%)
  blocking collectives  59.1 us (5%)
    ppermute x32, waiting for transfers between devices, from_behind(): lax.ppermute(array, axis, [(i, (i + by) % devices) for i in range(devices)])  398 us
    reduce_or x64, other arithmetic, tile_residual(): jnp.any(positives[:, :, None] == label_ids[None, None, :], axis=1)  252 us
    gather x64, local copies, waits for them, and re-layouts, one_block(): chosen = jnp.take(tile_split, block_rows, axis=1)  223 us
    dot_general x64, matrix products, one_block(): jnp.einsum('rsk,rt->skt', chosen, block_resid, preferred_element_type=jnp...  123 us
    dynamic_slice x128, local copies, waits for them, and re-layouts, block_both(): return lax.map(one_block, (row_ids, slot_counts, tiles_now, label_base))  85.2 us
    and x64, other arithmetic, one_block(): chosen = jnp.take(tile_split, block_rows, axis=1)  44.8 us
    add x64, other arithmetic, tile_residual(): label_ids = block_base + jnp.arange(tile_side, dtype=jnp.int32)  44.2 us
    all_gather x1, blocking collectives, local(): lax.all_gather(tile_rows, 'blk', axis=0, tiled=True)  38.9 us
  transfers between devices with their start and end apart: 32, of which 16 were waited for; matrix products, arithmetic and copies ran while one was open for 0% of the time, Pallas kernels for 0%

commit v1 on v0

v1 whole, which is shorter than its diff:
```python
import functools
import math

import jax
import jax.numpy as jnp
from jax import lax
from jax.experimental import pallas as pl
from jax.experimental.pallas import tpu as pltpu
from jax.sharding import PartitionSpec as P

beta_one = 0.9
beta_two = 0.999
adam_eps = 1e-08
learn_rate = 0.1
correction_one = 1.0 - 0.9**10
correction_two = 1.0 - 0.999**10

STEPS = 8.0
TOP = 32000.0
LN2 = math.log(2.0)
CODE_ROWS = 16
FIELDS = 8


def z_shift(array, by, z_size):
    moves = [(2 * z + h, 2 * ((z + by) % z_size) + h) for z in range(z_size) for h in range(2)]
    return lax.ppermute(array, "blk", moves)


def cross_moves(z_size, label_size):
    return [
        ((2 * z + h) * label_size + l, (2 * z + 1 - h) * label_size + (l ^ 2))
        for z in range(z_size)
        for h in range(2)
        for l in range(label_size)
    ]


def grad_kernel(with_acc, first, table, x0, x1, x2, x3, pos, w, *rest):
    acc, out = rest if with_acc else (None, rest[0])
    here = first + pl.program_id(0)
    base = table[here * FIELDS + 4]
    x = jnp.concatenate([x0[...], x1[...], x2[...], x3[...]], axis=1)
    w_t = w[0].T
    logits = lax.dot_general(w_t, x, (((1,), (1,)), ((), ())), preferred_element_type=jnp.float32)
    rel = pos[...] - base
    word_of = rel >> 5
    bit = jnp.left_shift(jnp.int32(1), rel & 31)
    sub = lax.broadcasted_iota(jnp.int32, rel.shape, 0)
    hits = []
    for word in range(4):
        m = jnp.where(word_of == word, bit, 0)
        for by in (4, 2, 1):
            m = m | pltpu.roll(m, by, 0)
        for part in range(4):
            hits.append(lax.shift_right_logical(m, sub + 8 * part) & 1)
    targets = jnp.concatenate(hits, axis=0).astype(jnp.float32)
    resid = (1.0 / (1.0 + jnp.exp(-logits)) - targets).astype(jnp.bfloat16)
    grad = jnp.dot(resid, x, preferred_element_type=jnp.float32)
    out[0] = grad if acc is None else acc[0] + grad


def tile_grad(table, x, pos, w, first, acc=None, acc_first=0):
    rows = x.shape[0]
    blocks, depth, side = w.shape
    slot_specs = [
        pl.BlockSpec((rows, side), functools.partial(lambda s, b, t: (0, t[(first + b) * FIELDS + s]), s))
        for s in range(4)
    ]
    specs = slot_specs + [
        pl.BlockSpec(pos.shape, lambda b, t: (0, 0)),
        pl.BlockSpec((1, depth, side), lambda b, t: (b, 0, 0)),
    ]
    operands = [x, x, x, x, pos, w]
    if acc is not None:
        specs.append(pl.BlockSpec((1, side, depth), lambda b, t: (b + acc_first, 0, 0)))
        operands.append(acc)
    return pl.pallas_call(
        functools.partial(grad_kernel, acc is not None, first),
        out_shape=jax.ShapeDtypeStruct((blocks, side, depth), jnp.float32),
        grid_spec=pltpu.PrefetchScalarGridSpec(
            num_scalar_prefetch=1,
            grid=(blocks,),
            in_specs=specs,
            out_specs=pl.BlockSpec((1, side, depth), lambda b, t: (b, 0, 0)),
        ),
        compiler_params=pltpu.CompilerParams(vmem_limit_bytes=32 * 1024 * 1024),
        cost_estimate=pl.CostEstimate(
            flops=8 * blocks * rows * depth * side,
            bytes_accessed=2 * blocks * rows * depth,
            transcendentals=2 * blocks * rows * side,
        ),
        name="tile_grad",
    )(table, *operands)


def decoded(q, codes):
    scale = jnp.exp(codes.astype(jnp.float32) * (LN2 / STEPS)) * (1.0 / TOP)
    return q.astype(jnp.int32).astype(jnp.float32) * scale


def encode_kernel(with_got, *refs):
    grad, out = refs[-2], refs[-1]
    side = grad.shape[1]
    total = 2 * side
    row = lax.broadcasted_iota(jnp.int32, (CODE_ROWS, grad.shape[2]), 0)
    codes = jnp.zeros((CODE_ROWS, grad.shape[2]), jnp.int32)
    if with_got:
        got = refs[0]
        got_codes = got[total : total + CODE_ROWS, :].astype(jnp.int32)
    for b in range(2):
        g = grad[b]
        if with_got:
            g = g + decoded(got[side * b : side * (b + 1), :], got_codes[b : b + 1])
        top = jnp.maximum(jnp.max(jnp.abs(g), axis=0, keepdims=True), 1e-30)
        code = jnp.ceil(jnp.log(top) * (STEPS / LN2))
        q = jnp.round(g * (jnp.exp(code * (-LN2 / STEPS)) * TOP))
        out[side * b : side * (b + 1), :] = q.astype(jnp.int32).astype(jnp.int16)
        codes = jnp.where(row == b, code.astype(jnp.int32), codes)
    out[total : total + CODE_ROWS, :] = codes.astype(jnp.int16)


def encode(grad, half, got=None):
    side, depth = grad.shape[1:]
    rows = 2 * side + CODE_ROWS
    whole = pl.BlockSpec((rows, depth), lambda i: (0, 0))
    specs = [pl.BlockSpec((2, side, depth), lambda i: (half, 0, 0))]
    operands = [grad]
    if got is not None:
        specs.insert(0, whole)
        operands.insert(0, got)
    return pl.pallas_call(
        functools.partial(encode_kernel, got is not None),
        out_shape=jax.ShapeDtypeStruct((rows, depth), jnp.int16),
        grid=(1,),
        in_specs=specs,
        out_specs=whole,
        compiler_params=pltpu.CompilerParams(vmem_limit_bytes=32 * 1024 * 1024),
        cost_estimate=pl.CostEstimate(flops=20 * rows * depth, bytes_accessed=8 * rows * depth, transcendentals=0),
        name="encode",
    )(*operands)


def adam_kernel(table, grad, low_a, low_b, high_a, high_b, weight, first, second, new_weight, new_first, new_second):
    b = pl.program_id(0)
    side = grad.shape[1]
    second_half, odd = b >= 2, b % 2
    start = pl.multiple_of(odd * side, side)
    total = grad[0]
    for first_msg, second_msg in ((low_a, low_b), (high_a, high_b)):
        q = jnp.where(
            second_half,
            second_msg[pl.ds(start, side), :].astype(jnp.int32),
            first_msg[pl.ds(start, side), :].astype(jnp.int32),
        )
        codes = jnp.where(
            second_half,
            second_msg[2 * side : 2 * side + CODE_ROWS, :].astype(jnp.int32),
            first_msg[2 * side : 2 * side + CODE_ROWS, :].astype(jnp.int32),
        )
        total = total + decoded(q, jnp.where(odd == 1, codes[1:2], codes[0:1]))
    count = table[b * FIELDS + 5]
    for s in range(4):
        g = total[:, s * side : (s + 1) * side].T
        kept = s < count
        m, v, w = first[0, s], second[0, s], weight[0, s]
        moved_first = beta_one * m + (1.0 - beta_one) * g
        moved_second = beta_two * v + (1.0 - beta_two) * g * g
        step_dir = moved_first / correction_one / (jnp.sqrt(moved_second / correction_two) + adam_eps)
        new_first[0, s] = jnp.where(kept, moved_first, m)
        new_second[0, s] = jnp.where(kept, moved_second, v)
        new_weight[0, s] = jnp.where(kept, w - learn_rate * step_dir, w)


def adam(table, grad, low_a, low_b, high_a, high_b, weight, first, second):
    blocks, slots, side = weight.shape[:3]
    msg = pl.BlockSpec(low_a.shape, lambda b, t: (0, 0))
    state = pl.BlockSpec((1,) + weight.shape[1:], lambda b, t: (b, 0, 0, 0))
    out = jax.ShapeDtypeStruct(weight.shape, jnp.float32)
    return pl.pallas_call(
        adam_kernel,
        out_shape=(out, out, out),
        grid_spec=pltpu.PrefetchScalarGridSpec(
            num_scalar_prefetch=1,
            grid=(blocks,),
            in_specs=[pl.BlockSpec((1, side, slots * side), lambda b, t: (b, 0, 0))] + [msg] * 4 + [state] * 3,
            out_specs=(state, state, state),
        ),
        compiler_params=pltpu.CompilerParams(vmem_limit_bytes=32 * 1024 * 1024),
        name="adam",
    )(table, grad, low_a, low_b, high_a, high_b, weight, first, second)


def local(features, positives, tile_rows, tile_count, weight, first_moment, second_moment):
    blocks, slots, side = weight.shape[:3]
    rows = features.shape[0]
    z_size = lax.axis_size("blk") // 2
    label_size = lax.axis_size("labels")
    shift = functools.partial(z_shift, z_size=z_size)
    blk, label = lax.axis_index("blk"), lax.axis_index("labels")
    crossing = cross_moves(z_size, label_size)

    with jax.named_scope("tables"):
        base = ((label * lax.axis_size("blk") + blk) * blocks + jnp.arange(blocks, dtype=jnp.int32)) * side
        fields = [tile_rows, base[:, None], tile_count[:, None], jnp.zeros((blocks, 2), jnp.int32)]
        own_table = jnp.concatenate(fields, axis=1)[None]
        table = own_table
        for by in (1, 2, 4):
            table = jnp.concatenate([table, shift(table, by)], axis=0)
        table = table.reshape(-1)
        own_table = own_table.reshape(-1)

    with jax.named_scope("rows_of_other_half"):
        part = rows // label_size
        piece = lax.dynamic_slice_in_dim(features, (label ^ 2) * part, part, 0)
        piece = lax.ppermute(piece, ("blk", "labels"), crossing)
        other = lax.all_gather(piece, "labels", axis=0, tiled=True)
        own_pos = positives.T
        other_pos = lax.ppermute(own_pos, ("blk", "labels"), crossing)

    with jax.named_scope("kept_tiles"):
        kept = jnp.arange(slots, dtype=jnp.int32)[None, :] < tile_count[:, None]
        tiles = jnp.where(kept[:, :, None, None], weight, 0.0).astype(jnp.bfloat16)
        tiles = tiles.reshape(blocks, slots * side, side)

    with jax.named_scope("tiles_round_z"):
        ring = {0: tiles}
        up, down = tiles, tiles
        for hop in (1, 2, 3):
            up, down = shift(up, 1), shift(down, -1)
            ring[hop], ring[z_size - hop] = up, down
        far = (shift(up[:2], 1), shift(down[2:], -1))

    with jax.named_scope("own_rows"):
        part_sum = {}
        for j in (0, 1, 7, 2, 6, 3, 5):
            part_sum[j] = tile_grad(table, features, own_pos, ring[j], j * blocks)
        far_sum = [tile_grad(table, features, own_pos, far[i], 4 * blocks + 2 * i) for i in range(2)]

    with jax.named_scope("other_rows"):
        full = {}
        far_full = [
            tile_grad(table, other, other_pos, far[i], 4 * blocks + 2 * i, far_sum[i]) for i in range(2)
        ]
        for j in (5, 3, 6, 2, 7, 1, 0):
            full[j] = tile_grad(table, other, other_pos, ring[j], j * blocks, part_sum[j])

    with jax.named_scope("sums_round_z"):
        down_a, up_b = encode(far_full[0], 0), encode(far_full[1], 0)
        down_b = up_a = None
        for hop in (3, 2, 1):
            down_a, up_b = shift(down_a, -1), shift(up_b, 1)
            if down_b is not None:
                down_b, up_a = shift(down_b, -1), shift(up_a, 1)
            down_b, up_a = encode(full[hop], 1, down_b), encode(full[z_size - hop], 0, up_a)
            down_a, up_b = encode(full[hop], 0, down_a), encode(full[z_size - hop], 1, up_b)
        down_a, up_b = shift(down_a, -1), shift(up_b, 1)
        down_b, up_a = shift(down_b, -1), shift(up_a, 1)

    with jax.named_scope("adam"):
        return tuple(
            adam(own_table, full[0], down_a, down_b, up_a, up_b, weight, first_moment, second_moment)
        )


def solution(mesh):
    whole = P(("labels", "blk"), None, None, None)
    return jax.shard_map(
        local,
        mesh=mesh,
        in_specs=(
            P("blk", None),
            P("blk", None),
            P(("labels", "blk"), None),
            P(("labels", "blk")),
            whole,
            whole,
            whole,
        ),
        out_specs=(whole, whole, whole),
        check_vma=False,
    )
```

time: 1300 us -> 194 us (0.15)
  waiting for transfers between devices: 398 us -> 31.4 us
  other arithmetic: 364 us -> 3.64 us
  local copies, waits for them, and re-layouts: 342 us -> 18.3 us
  matrix products: 123 us -> 0 us
  Pallas kernels: 0 us -> 79.9 us
  blocking collectives: 59.1 us -> 0 us
  starting transfers between devices: 4.27 us -> 45.2 us
  between operations: 1.35 us -> 14.7 us
    ppermute x32 -> x27, waiting for transfers between devices: 398 us -> 31.4 us  [the longest x25 22.3 us: z_shift(): return lax.ppermute(array, 'blk', moves)]
    reduce_or x64 -> x0, other arithmetic: 252 us -> none  [tile_residual(): jnp.any(positives[:, :, None] == label_ids[None, None, :], axis=1)]
    gather x64 -> x0, local copies, waits for them, and re-layouts: 223 us -> none  [one_block(): chosen = jnp.take(tile_split, block_rows, axis=1)]
    dot_general x64 -> x0, matrix products: 123 us -> none  [one_block(): jnp.einsum('rsk,rt->skt', chosen, block_resid, preferred_element_type=jnp...]
    dynamic_slice x160 -> x1, local copies, waits for them, and re-layouts: 86.5 us -> 1.03 us  [local(): piece = lax.dynamic_slice_in_dim(features, (label ^ 2) * part, part, 0)]
    pallas_call x0 -> x33, Pallas kernels: none -> 79.9 us  [the longest x18 74.5 us: tile_grad(): pl.pallas_call(functools.partial(grad_kernel, acc is not None, first), ou...]
    add x96 -> x0, other arithmetic: 61.6 us -> none  [the longest x64 44.2 us: tile_residual(): label_ids = block_base + jnp.arange(tile_side, dtype=jnp.int32)]
    and x64 -> x0, other arithmetic: 44.8 us -> none  [one_block(): chosen = jnp.take(tile_split, block_rows, axis=1)]
  transfers between devices with their start and end apart: 32 -> 28, of which waited for: 16 -> 4; matrix products, arithmetic and copies ran while one was open for 0% -> 2% of each run, Pallas kernels for 0% -> 38%
where the time goes in v1:
time: 194 us; the launch traced here: 193 us
  Pallas kernels  79.9 us (41%)
  starting transfers between devices  45.2 us (23%)
  waiting for transfers between devices  31.4 us (16%)
  local copies, waits for them, and re-layouts  18.3 us (9%)
  between operations  14.7 us (8%)
  other arithmetic  3.64 us (2%)
    pallas_call x18, Pallas kernels, tile_grad(): pl.pallas_call(functools.partial(grad_kernel, acc is not None, first), ou...  74.5 us
    ppermute x25, starting transfers between devices, z_shift(): return lax.ppermute(array, 'blk', moves)  39.1 us
    ppermute x25, waiting for transfers between devices, z_shift(): return lax.ppermute(array, 'blk', moves)  22.3 us
    unnamed x64, local copies, waits for them, and re-layouts  16.2 us
    ppermute x1, waiting for transfers between devices, local(): piece = lax.ppermute(piece, ('blk', 'labels'), crossing)  9.11 us
  transfers between devices with their start and end apart: 28, of which 4 were waited for; matrix products, arithmetic and copies ran while one was open for 2% of the time, Pallas kernels for 38%

profile of v1, /device:TPU:4, one launch (start us, length us, event | category | flops | bytes accessed | tf_op | source)
XLA Modules:
  0.0 193.1 jit_solution(13456302341614787735)
XLA Ops:
  7.2 1.0 constant_dynamic-slice_fusion
  8.2 3.1 %collective-permute-start.3 = (bf16[48,4096]{1,0:T(8,128)(2,1)S(1)}, bf16[48,4096]{1,0:T(8,128)(2,1)S(1)}, u32[]{:S(2)}, u32[]{:S(2)}) collective-permute-start(bf16[48,4096]{1,0:T(8,128)(2,1)S(1)} %constant_dynamic-slice_fusion), channel_id=1, source_target_pairs={{0,18},{1,19},{2,16},{3,17},{4,22},{5,23},{6,20},{7,21},{8,26},{9,... | collective-permute-start | bytes 1179656 | tf_op jit(solution)/shard_map/rows_of_other_half/ppermute | solution.py:216
  11.4 9.1 %collective-permute-done.3 = bf16[48,4096]{1,0:T(8,128)(2,1)S(1)} collective-permute-done((bf16[48,4096]{1,0:T(8,128)(2,1)S(1)}, bf16[48,4096]{1,0:T(8,128)(2,1)S(1)}, u32[]{:S(2)}, u32[]{:S(2)}) %collective-permute-start.3) | collective-permute-done | bytes 393248 | tf_op jit(solution)/shard_map/rows_of_other_half/ppermute | solution.py:216
  21.9 1.4 select_convert_fusion
  23.3 5.9 %collective-permute-start.16 = (bf16[4,512,128]{2,1,0:T(8,128)(2,1)S(1)}, bf16[4,512,128]{2,1,0:T(8,128)(2,1)S(1)}, u32[]{:S(2)}, u32[]{:S(2)}) collective-permute-start(bf16[4,512,128]{2,1,0:T(8,128)(2,1)S(1)} %bitcast.7), channel_id=1, source_target_pairs={{0,224},{16,240},{32,0},{48,16},{64,32},{80,48},{96,64},{112,80},{... | collective-permute-start | bytes 1572872 | tf_op jit(solution)/shard_map/tiles_round_z/ppermute | solution.py:27
  30.9 8.8 %collective-permute-done.16.w = bf16[4,512,128]{2,1,0:T(8,128)(2,1)S(1)} collective-permute-done((bf16[4,512,128]{2,1,0:T(8,128)(2,1)S(1)}, bf16[4,512,128]{2,1,0:T(8,128)(2,1)S(1)}, u32[]{:S(2)}, u32[]{:S(2)}) %collective-permute-start.16) | collective-permute-done | bytes 524320 | tf_op jit(solution)/shard_map/tiles_round_z/ppermute | solution.py:27
  39.7 3.7 %collective-permute-start.17 = (bf16[4,512,128]{2,1,0:T(8,128)(2,1)S(1)}, bf16[4,512,128]{2,1,0:T(8,128)(2,1)}, u32[]{:S(2)}, u32[]{:S(2)}) collective-permute-start(bf16[4,512,128]{2,1,0:T(8,128)(2,1)S(1)} %collective-permute-done.16.w), channel_id=1, source_target_pairs={{0,224},{16,240},{32,0},{48,16},{64,32},{80,48},{96,64},{112,80},{... | collective-permute-start | bytes 1572872 | tf_op jit(solution)/shard_map/tiles_round_z/ppermute | solution.py:27
  44.3 3.0 %collective-permute-start.4 = (s32[8,768]{1,0:T(8,128)}, s32[8,768]{1,0:T(8,128)S(1)}, u32[]{:S(2)}, u32[]{:S(2)}) collective-permute-start(s32[8,768]{1,0:T(8,128)} %bitcast.11), channel_id=1, source_target_pairs={{0,18},{1,19},{2,16},{3,17},{4,22},{5,23},{6,20},{7,21},{8,26},{9,... | collective-permute-start | bytes 73736 | tf_op jit(solution)/shard_map/rows_of_other_half/ppermute | solution.py:219
  47.3 8.5 %collective-permute-done.1 = s32[2,4,8]{2,1,0:T(4,128)S(1)} collective-permute-done((s32[2,4,8]{2,1,0:T(4,128)S(1)}, s32[2,4,8]{2,1,0:T(4,128)S(1)}, u32[]{:S(2)}, u32[]{:S(2)}) %collective-permute-start.1) | collective-permute-done | bytes 288 | tf_op jit(solution)/shard_map/tables/ppermute | solution.py:27
  55.8 1.8 collective-permute-start.2
  58.5 4.9 %collective-permute-done.2 = s32[4,4,8]{2,1,0:T(4,128)S(1)} collective-permute-done((s32[4,4,8]{2,1,0:T(4,128)S(1)}, s32[4,4,8]{2,1,0:T(4,128)S(1)}, u32[]{:S(2)}, u32[]{:S(2)}) %collective-permute-start.2) | collective-permute-done | bytes 544 | tf_op jit(solution)/shard_map/tables/ppermute | solution.py:27
  63.5 1.1 collective-permute-start.18
  64.7 2.0 %collective-permute-start.7 = (bf16[4,512,128]{2,1,0:T(8,128)(2,1)}, bf16[4,512,128]{2,1,0:T(8,128)(2,1)S(1)}, u32[]{:S(2)}, u32[]{:S(2)}) collective-permute-start(bf16[4,512,128]{2,1,0:T(8,128)(2,1)} %collective-permute-done.6.w), channel_id=1, source_target_pairs={{0,32},{16,48},{32,64},{48,80},{64,96},{80,112},{96,128},{112,144}... | collective-permute-start | bytes 1572872 | tf_op jit(solution)/shard_map/tiles_round_z/ppermute | solution.py:27
  66.7 2.8 %copy-done = bf16[768,4096]{1,0:T(8,128)(2,1)S(1)} copy-done((bf16[768,4096]{1,0:T(8,128)(2,1)S(1)}, bf16[768,4096]{1,0:T(8,128)(2,1)}, u32[]{:S(2)}) %copy-start) | copy-done | bytes 6291480
  70.3 4.3 %tile_grad.26.rest_0_ = f32[4,128,512]{2,1,0:T(8,128)S(1)} custom-call(s32[256]{0:T(256)S(1)} %reshape.43.table, bf16[768,4096]{1,0:T(8,128)(2,1)S(1)} %copy-done, bf16[768,4096]{1,0:T(8,128)(2,1)S(1)} %copy-done, bf16[768,4096]{1,0:T(8,128)(2,1)S(1)} %copy-done, bf16[768,4096]{1,0:T(8,128)(2,1)S(1)} %copy-done, s32[8,768]{1,0:T(8,128)S(1)} %bitcast.12, ...), custom_call_target="tpu_custom_call" | custom-call | flops 1610612736 | bytes 3145728 | tf_op jit(solution)/shard_map/own_rows/tile_grad/pallas_call | solution.py:78
  75.4 4.4 %tile_grad.32.rest_0_ = f32[4,128,512]{2,1,0:T(8,128)S(1)} custom-call(s32[256]{0:T(256)S(1)} %reshape.43.table, bf16[768,4096]{1,0:T(8,128)(2,1)S(1)} %copy-done, bf16[768,4096]{1,0:T(8,128)(2,1)S(1)} %copy-done, bf16[768,4096]{1,0:T(8,128)(2,1)S(1)} %copy-done, bf16[768,4096]{1,0:T(8,128)(2,1)S(1)} %copy-done, s32[8,768]{1,0:T(8,128)S(1)} %bitcast.13, ...), custom_call_target="tpu_custom_call" | custom-call | flops 1610612736 | bytes 3145728 | tf_op jit(solution)/shard_map/own_rows/tile_grad/pallas_call | solution.py:78
  79.8 5.2 %tile_grad.24.rest_0_ = f32[4,128,512]{2,1,0:T(8,128)S(1)} custom-call(s32[256]{0:T(256)S(1)} %reshape.43.table, bf16[768,4096]{1,0:T(8,128)(2,1)S(1)} %copy-done, bf16[768,4096]{1,0:T(8,128)(2,1)S(1)} %copy-done, bf16[768,4096]{1,0:T(8,128)(2,1)S(1)} %copy-done, bf16[768,4096]{1,0:T(8,128)(2,1)S(1)} %copy-done, s32[8,768]{1,0:T(8,128)S(1)} %bitcast.14, ...), custom_call_target="tpu_custom_call" | custom-call | flops 1610612736 | bytes 3145728 | tf_op jit(solution)/shard_map/own_rows/tile_grad/pallas_call | solution.py:78
  85.0 1.0 copy-done.5
  86.0 5.2 %tile_grad.30.rest_0_ = f32[4,128,512]{2,1,0:T(8,128)S(1)} custom-call(s32[256]{0:T(256)S(1)} %reshape.43.table, bf16[768,4096]{1,0:T(8,128)(2,1)S(1)} %copy-done, bf16[768,4096]{1,0:T(8,128)(2,1)S(1)} %copy-done, bf16[768,4096]{1,0:T(8,128)(2,1)S(1)} %copy-done, bf16[768,4096]{1,0:T(8,128)(2,1)S(1)} %copy-done, s32[8,768]{1,0:T(8,128)S(1)} %bitcast.15, ...), custom_call_target="tpu_custom_call" | custom-call | flops 1610612736 | bytes 3145728 | tf_op jit(solution)/shard_map/own_rows/tile_grad/pallas_call | solution.py:78
  91.2 1.0 copy-done.3
  92.2 1.3 collective-permute-start.22
  93.6 1.0 collective-permute-start.8
  94.6 4.3 %tile_grad.22.rest_0_ = f32[4,128,512]{2,1,0:T(8,128)S(1)} custom-call(s32[256]{0:T(256)S(1)} %reshape.43.table, bf16[768,4096]{1,0:T(8,128)(2,1)S(1)} %copy-done, bf16[768,4096]{1,0:T(8,128)(2,1)S(1)} %copy-done, bf16[768,4096]{1,0:T(8,128)(2,1)S(1)} %copy-done, bf16[768,4096]{1,0:T(8,128)(2,1)S(1)} %copy-done, s32[8,768]{1,0:T(8,128)S(1)} %bitcast.16, ...), custom_call_target="tpu_custom_call" | custom-call | flops 1610612736 | bytes 3145728 | tf_op jit(solution)/shard_map/own_rows/tile_grad/pallas_call | solution.py:78
  99.0 1.0 copy-done.9
  99.9 4.3 %tile_grad.28.rest_0_ = f32[4,128,512]{2,1,0:T(8,128)S(1)} custom-call(s32[256]{0:T(256)S(1)} %reshape.43.table, bf16[768,4096]{1,0:T(8,128)(2,1)S(1)} %copy-done, bf16[768,4096]{1,0:T(8,128)(2,1)S(1)} %copy-done, bf16[768,4096]{1,0:T(8,128)(2,1)S(1)} %copy-done, bf16[768,4096]{1,0:T(8,128)(2,1)S(1)} %copy-done, s32[8,768]{1,0:T(8,128)S(1)} %bitcast.17, ...), custom_call_target="tpu_custom_call" | custom-call | flops 1610612736 | bytes 3145728 | tf_op jit(solution)/shard_map/own_rows/tile_grad/pallas_call | solution.py:78
  105.2 2.5 %tile_grad.34.rest_0_ = f32[2,128,512]{2,1,0:T(8,128)S(1)} custom-call(s32[256]{0:T(256)S(1)} %reshape.43.table, bf16[768,4096]{1,0:T(8,128)(2,1)S(1)} %copy-done, bf16[768,4096]{1,0:T(8,128)(2,1)S(1)} %copy-done, bf16[768,4096]{1,0:T(8,128)(2,1)S(1)} %copy-done, bf16[768,4096]{1,0:T(8,128)(2,1)S(1)} %copy-done, s32[8,768]{1,0:T(8,128)S(1)} %bitcast.18, ...), custom_call_target="tpu_custom_call" | custom-call | flops 805306368 | bytes 1572864 | tf_op jit(solution)/shard_map/own_rows/tile_grad/pallas_call | solution.py:78
  108.5 2.5 %tile_grad.20.rest_0_ = f32[2,128,512]{2,1,0:T(8,128)S(1)} custom-call(s32[256]{0:T(256)S(1)} %reshape.43.table, bf16[768,4096]{1,0:T(8,128)(2,1)S(1)} %copy-done, bf16[768,4096]{1,0:T(8,128)(2,1)S(1)} %copy-done, bf16[768,4096]{1,0:T(8,128)(2,1)S(1)} %copy-done, bf16[768,4096]{1,0:T(8,128)(2,1)S(1)} %copy-done, s32[8,768]{1,0:T(8,128)S(1)} %bitcast.19, ...), custom_call_target="tpu_custom_call" | custom-call | flops 805306368 | bytes 1572864 | tf_op jit(solution)/shard_map/own_rows/tile_grad/pallas_call | solution.py:78
  111.9 2.8 %copy-done.1 = bf16[768,4096]{1,0:T(8,128)(2,1)S(1)} copy-done((bf16[768,4096]{1,0:T(8,128)(2,1)S(1)}, bf16[768,4096]{1,0:T(8,128)(2,1)}, u32[]{:S(2)}) %copy-start.1) | copy-done | bytes 6291480
  114.6 1.0 copy-done.22
  116.6 2.5 %tile_grad.35.refs_0_ = f32[2,128,512]{2,1,0:T(8,128)S(1)} custom-call(s32[256]{0:T(256)S(1)} %reshape.43.table, bf16[768,4096]{1,0:T(8,128)(2,1)S(1)} %copy-done.1, bf16[768,4096]{1,0:T(8,128)(2,1)S(1)} %copy-done.1, bf16[768,4096]{1,0:T(8,128)(2,1)S(1)} %copy-done.1, bf16[768,4096]{1,0:T(8,128)(2,1)S(1)} %copy-done.1, ...), custom_call_target="tpu_custom_call" | custom-call | flops 805306368 | bytes 1572864 | tf_op jit(solution)/shard_map/other_rows/tile_grad/pallas_call | solution.py:78
  119.3 2.0 %collective-permute-start.23 = (s16[272,512]{1,0:T(8,128)(2,1)S(1)}, s16[272,512]{1,0:T(8,128)(2,1)S(1)}, u32[]{:S(2)}, u32[]{:S(2)}) collective-permute-start(s16[272,512]{1,0:T(8,128)(2,1)S(1)} %encode.24), channel_id=1, source_target_pairs={{0,32},{16,48},{32,64},{48,80},{64,96},{80,112},{96,128},{112,144}... | collective-permute-start | bytes 835592 | tf_op jit(solution)/shard_map/sums_round_z/ppermute | solution.py:27
  121.3 2.5 %tile_grad.21.refs_0_ = f32[2,128,512]{2,1,0:T(8,128)S(1)} custom-call(s32[256]{0:T(256)S(1)} %reshape.43.table, bf16[768,4096]{1,0:T(8,128)(2,1)S(1)} %copy-done.2, bf16[768,4096]{1,0:T(8,128)(2,1)S(1)} %copy-done.2, bf16[768,4096]{1,0:T(8,128)(2,1)S(1)} %copy-done.2, bf16[768,4096]{1,0:T(8,128)(2,1)S(1)} %copy-done.2, ...), custom_call_target="tpu_custom_call" | custom-call | flops 805306368 | bytes 1572864 | tf_op jit(solution)/shard_map/other_rows/tile_grad/pallas_call | solution.py:78
  123.9 1.3 collective-permute-start.9
  125.3 4.3 %tile_grad.23.refs_1_.refs_0_ = f32[4,128,512]{2,1,0:T(8,128)S(1)} custom-call(s32[256]{0:T(256)S(1)} %reshape.43.table, bf16[768,4096]{1,0:T(8,128)(2,1)S(1)} %copy-done.2, bf16[768,4096]{1,0:T(8,128)(2,1)S(1)} %copy-done.2, bf16[768,4096]{1,0:T(8,128)(2,1)S(1)} %copy-done.2, bf16[768,4096]{1,0:T(8,128)(2,1)S(1)} %copy-done.2, ...), custom_call_target="tpu_custom_call" | custom-call | flops 1610612736 | bytes 3145728 | tf_op jit(solution)/shard_map/other_rows/tile_grad/pallas_call | solution.py:78
  129.7 1.4 collective-permute-start.13
  131.1 4.3 %tile_grad.29.refs_0_.refs_1_ = f32[4,128,512]{2,1,0:T(8,128)S(1)} custom-call(s32[256]{0:T(256)S(1)} %reshape.43.table, bf16[768,4096]{1,0:T(8,128)(2,1)S(1)} %copy-done.2, bf16[768,4096]{1,0:T(8,128)(2,1)S(1)} %copy-done.2, bf16[768,4096]{1,0:T(8,128)(2,1)S(1)} %copy-done.2, bf16[768,4096]{1,0:T(8,128)(2,1)S(1)} %copy-done.2, ...), custom_call_target="tpu_custom_call" | custom-call | flops 1610612736 | bytes 3145728 | tf_op jit(solution)/shard_map/other_rows/tile_grad/pallas_call | solution.py:78
  136.6 2.6 %collective-permute-start.10 = (s16[272,512]{1,0:T(8,128)(2,1)S(1)}, s16[272,512]{1,0:T(8,128)(2,1)S(1)}, u32[]{:S(2)}, u32[]{:S(2)}) collective-permute-start(s16[272,512]{1,0:T(8,128)(2,1)S(1)} %encode.15), channel_id=1, source_target_pairs={{0,224},{16,240},{32,0},{48,16},{64,32},{80,48},{96,64},{112,80},{... | collective-permute-start | bytes 835592 | tf_op jit(solution)/shard_map/sums_round_z/ppermute | solution.py:27
  139.7 5.3 %tile_grad.25.refs_1_ = f32[4,128,512]{2,1,0:T(8,128)S(1)} custom-call(s32[256]{0:T(256)S(1)} %reshape.43.table, bf16[768,4096]{1,0:T(8,128)(2,1)S(1)} %copy-done.2, bf16[768,4096]{1,0:T(8,128)(2,1)S(1)} %copy-done.2, bf16[768,4096]{1,0:T(8,128)(2,1)S(1)} %copy-done.2, bf16[768,4096]{1,0:T(8,128)(2,1)S(1)} %copy-done.2, ...), custom_call_target="tpu_custom_call" | custom-call | flops 1610612736 | bytes 3145728 | tf_op jit(solution)/shard_map/other_rows/tile_grad/pallas_call | solution.py:78
  144.9 5.3 %tile_grad.31.refs_1_ = f32[4,128,512]{2,1,0:T(8,128)S(1)} custom-call(s32[256]{0:T(256)S(1)} %reshape.43.table, bf16[768,4096]{1,0:T(8,128)(2,1)S(1)} %copy-done.2, bf16[768,4096]{1,0:T(8,128)(2,1)S(1)} %copy-done.2, bf16[768,4096]{1,0:T(8,128)(2,1)S(1)} %copy-done.2, bf16[768,4096]{1,0:T(8,128)(2,1)S(1)} %copy-done.2, ...), custom_call_target="tpu_custom_call" | custom-call | flops 1610612736 | bytes 3145728 | tf_op jit(solution)/shard_map/other_rows/tile_grad/pallas_call | solution.py:78
  150.4 3.3 %collective-permute-start.14 = (s16[272,512]{1,0:T(8,128)(2,1)S(1)}, s16[272,512]{1,0:T(8,128)(2,1)S(1)}, u32[]{:S(2)}, u32[]{:S(2)}) collective-permute-start(s16[272,512]{1,0:T(8,128)(2,1)S(1)} %encode.19), channel_id=1, source_target_pairs={{0,224},{16,240},{32,0},{48,16},{64,32},{80,48},{96,64},{112,80},{... | collective-permute-start | bytes 835592 | tf_op jit(solution)/shard_map/sums_round_z/ppermute | solution.py:27
  154.2 3.3 %collective-permute-start.11 = (s16[272,512]{1,0:T(8,128)(2,1)S(1)}, s16[272,512]{1,0:T(8,128)(2,1)S(1)}, u32[]{:S(2)}, u32[]{:S(2)}) collective-permute-start(s16[272,512]{1,0:T(8,128)(2,1)S(1)} %encode.16), channel_id=1, source_target_pairs={{0,224},{16,240},{32,0},{48,16},{64,32},{80,48},{96,64},{112,80},{... | collective-permute-start | bytes 835592 | tf_op jit(solution)/shard_map/sums_round_z/ppermute | solution.py:27
  157.8 4.3 %tile_grad.27.refs_1_ = f32[4,128,512]{2,1,0:T(8,128)S(1)} custom-call(s32[256]{0:T(256)S(1)} %reshape.43.table, bf16[768,4096]{1,0:T(8,128)(2,1)S(1)} %copy-done.2, bf16[768,4096]{1,0:T(8,128)(2,1)S(1)} %copy-done.2, bf16[768,4096]{1,0:T(8,128)(2,1)S(1)} %copy-done.2, bf16[768,4096]{1,0:T(8,128)(2,1)S(1)} %copy-done.2, ...), custom_call_target="tpu_custom_call" | custom-call | flops 1610612736 | bytes 3145728 | tf_op jit(solution)/shard_map/other_rows/tile_grad/pallas_call | solution.py:78
  162.1 4.4 %tile_grad.33.refs_1_ = f32[4,128,512]{2,1,0:T(8,128)S(1)} custom-call(s32[256]{0:T(256)S(1)} %reshape.43.table, bf16[768,4096]{1,0:T(8,128)(2,1)S(1)} %copy-done.2, bf16[768,4096]{1,0:T(8,128)(2,1)S(1)} %copy-done.2, bf16[768,4096]{1,0:T(8,128)(2,1)S(1)} %copy-done.2, bf16[768,4096]{1,0:T(8,128)(2,1)S(1)} %copy-done.2, ...), custom_call_target="tpu_custom_call" | custom-call | flops 1610612736 | bytes 3145728 | tf_op jit(solution)/shard_map/other_rows/tile_grad/pallas_call | solution.py:78
  166.7 3.3 %collective-permute-start.15 = (s16[272,512]{1,0:T(8,128)(2,1)S(1)}, s16[272,512]{1,0:T(8,128)(2,1)S(1)}, u32[]{:S(2)}, u32[]{:S(2)}) collective-permute-start(s16[272,512]{1,0:T(8,128)(2,1)S(1)} %encode.20), channel_id=1, source_target_pairs={{0,224},{16,240},{32,0},{48,16},{64,32},{80,48},{96,64},{112,80},{... | collective-permute-start | bytes 835592 | tf_op jit(solution)/shard_map/sums_round_z/ppermute | solution.py:27
  170.5 3.3 %collective-permute-start.12 = (s16[272,512]{1,0:T(8,128)(2,1)S(1)}, s16[272,512]{1,0:T(8,128)(2,1)S(1)}, u32[]{:S(2)}, u32[]{:S(2)}) collective-permute-start(s16[272,512]{1,0:T(8,128)(2,1)S(1)} %encode.17), channel_id=1, source_target_pairs={{0,224},{16,240},{32,0},{48,16},{64,32},{80,48},{96,64},{112,80},{... | collective-permute-start | bytes 835592 | tf_op jit(solution)/shard_map/sums_round_z/ppermute | solution.py:27
  174.1 4.4 %tile_grad.18.rest_0_ = f32[4,128,512]{2,1,0:T(8,128)S(1)} custom-call(s32[256]{0:T(256)S(1)} %reshape.43.table, bf16[768,4096]{1,0:T(8,128)(2,1)S(1)} %bitcast.6, bf16[768,4096]{1,0:T(8,128)(2,1)S(1)} %bitcast.6, bf16[768,4096]{1,0:T(8,128)(2,1)S(1)} %bitcast.6, bf16[768,4096]{1,0:T(8,128)(2,1)S(1)} %bitcast.6, s32[8,768]{1,0:T(8,128)S(1)} %bitcast.20, ...), custom_call_target="tpu_custom_call" | custom-call | flops 1610612736 | bytes 3145728 | tf_op jit(solution)/shard_map/own_rows/tile_grad/pallas_call | solution.py:78
  178.5 4.4 %tile_grad.19.grad = f32[4,128,512]{2,1,0:T(8,128)S(1)} custom-call(s32[256]{0:T(256)S(1)} %reshape.43.table, bf16[768,4096]{1,0:T(8,128)(2,1)S(1)} %copy-done.2, bf16[768,4096]{1,0:T(8,128)(2,1)S(1)} %copy-done.2, bf16[768,4096]{1,0:T(8,128)(2,1)S(1)} %copy-done.2, bf16[768,4096]{1,0:T(8,128)(2,1)S(1)} %copy-done.2, ...), custom_call_target="tpu_custom_call" | custom-call | flops 1610612736 | bytes 3145728 | tf_op jit(solution)/shard_map/other_rows/tile_grad/pallas_call | solution.py:78
  183.0 3.3 %adam.1 = (f32[4,4,128,128]{3,2,1,0:T(8,128)}, f32[4,4,128,128]{3,2,1,0:T(8,128)}, f32[4,4,128,128]{3,2,1,0:T(8,128)}) custom-call(s32[32]{0:T(128)S(1)} %broadcast_in_dim.26.table, f32[4,128,512]{2,1,0:T(8,128)S(1)} %tile_grad.19.grad, s16[272,512]{1,0:T(8,128)(2,1)S(1)} %collective-permute-done.12.low_a, ...), custom_call_target="tpu_custom_call" | custom-call | tf_op jit(solution)/shard_map/adam/adam/pallas_call | solution.py:180
  (123 shorter events, 13.8 us)
Async XLA Ops:
  7.2 104.7 %all-gather.2.cloned.1.call-start = ((), (), s32[]{:S(2)}) async-start(), calls=%async_computation | async-start | bytes 6684672 | tf_op jit(solution)/shard_map/rows_of_other_half/all_gather | solution.py:217
  8.2 12.2 %collective-permute-start.3 = (bf16[48,4096]{1,0:T(8,128)(2,1)S(1)}, bf16[48,4096]{1,0:T(8,128)(2,1)S(1)}, u32[]{:S(2)}, u32[]{:S(2)}) collective-permute-start(bf16[48,4096]{1,0:T(8,128)(2,1)S(1)} %constant_dynamic-slice_fusion), channel_id=1, source_target_pairs={{0,18},{1,19},{2,16},{3,17},{4,22},{5,23},{6,20},{7,21},{8,26},{9,... | collective-permute-start | bytes 1179656 | tf_op jit(solution)/shard_map/rows_of_other_half/ppermute | solution.py:216
  23.3 16.3 %collective-permute-start.16 = (bf16[4,512,128]{2,1,0:T(8,128)(2,1)S(1)}, bf16[4,512,128]{2,1,0:T(8,128)(2,1)S(1)}, u32[]{:S(2)}, u32[]{:S(2)}) collective-permute-start(bf16[4,512,128]{2,1,0:T(8,128)(2,1)S(1)} %bitcast.7), channel_id=1, source_target_pairs={{0,224},{16,240},{32,0},{48,16},{64,32},{80,48},{96,64},{112,80},{... | collective-permute-start | bytes 1572872 | tf_op jit(solution)/shard_map/tiles_round_z/ppermute | solution.py:27
  29.3 14.9 %collective-permute-start.5 = (bf16[4,512,128]{2,1,0:T(8,128)(2,1)S(1)}, bf16[4,512,128]{2,1,0:T(8,128)(2,1)S(1)}, u32[]{:S(2)}, u32[]{:S(2)}) collective-permute-start(bf16[4,512,128]{2,1,0:T(8,128)(2,1)S(1)} %bitcast.8), channel_id=1, source_target_pairs={{0,32},{16,48},{32,64},{48,80},{64,96},{80,112},{96,128},{112,144}... | collective-permute-start | bytes 1572872 | tf_op jit(solution)/shard_map/tiles_round_z/ppermute | solution.py:27
  30.9 13.3 %collective-permute-start = (s32[1,4,8]{2,1,0:T(4,128)S(1)}, s32[1,4,8]{2,1,0:T(4,128)S(1)}, u32[]{:S(2)}, u32[]{:S(2)}) collective-permute-start(s32[1,4,8]{2,1,0:T(4,128)S(1)} %fusion), channel_id=1, source_target_pairs={{0,32},{16,48},{32,64},{48,80},{64,96},{80,112},{96,128},{112,144}... | collective-permute-start | bytes 392 | tf_op jit(solution)/shard_map/tables/ppermute | solution.py:27
  39.7 23.8 %collective-permute-start.17 = (bf16[4,512,128]{2,1,0:T(8,128)(2,1)S(1)}, bf16[4,512,128]{2,1,0:T(8,128)(2,1)}, u32[]{:S(2)}, u32[]{:S(2)}) collective-permute-start(bf16[4,512,128]{2,1,0:T(8,128)(2,1)S(1)} %collective-permute-done.16.w), channel_id=1, source_target_pairs={{0,224},{16,240},{32,0},{48,16},{64,32},{80,48},{96,64},{112,80},{... | collective-permute-start | bytes 1572872 | tf_op jit(solution)/shard_map/tiles_round_z/ppermute | solution.py:27
  44.2 20.5 %collective-permute-start.6 = (bf16[4,512,128]{2,1,0:T(8,128)(2,1)S(1)}, bf16[4,512,128]{2,1,0:T(8,128)(2,1)}, u32[]{:S(2)}, u32[]{:S(2)}) collective-permute-start(bf16[4,512,128]{2,1,0:T(8,128)(2,1)S(1)} %collective-permute-done.5.w), channel_id=1, source_target_pairs={{0,32},{16,48},{32,64},{48,80},{64,96},{80,112},{96,128},{112,144}... | collective-permute-start | bytes 1572872 | tf_op jit(solution)/shard_map/tiles_round_z/ppermute | solution.py:27
  44.2 11.6 %collective-permute-start.1 = (s32[2,4,8]{2,1,0:T(4,128)S(1)}, s32[2,4,8]{2,1,0:T(4,128)S(1)}, u32[]{:S(2)}, u32[]{:S(2)}) collective-permute-start(s32[2,4,8]{2,1,0:T(4,128)S(1)} %pad_add_fusion.2), channel_id=1, source_target_pairs={{0,64},{16,80},{32,96},{48,112},{64,128},{80,144},{96,160},{112,17... | collective-permute-start | bytes 776 | tf_op jit(solution)/shard_map/tables/ppermute | solution.py:27
  44.3 67.5 %collective-permute-start.4 = (s32[8,768]{1,0:T(8,128)}, s32[8,768]{1,0:T(8,128)S(1)}, u32[]{:S(2)}, u32[]{:S(2)}) collective-permute-start(s32[8,768]{1,0:T(8,128)} %bitcast.11), channel_id=1, source_target_pairs={{0,18},{1,19},{2,16},{3,17},{4,22},{5,23},{6,20},{7,21},{8,26},{9,... | collective-permute-start | bytes 73736 | tf_op jit(solution)/shard_map/rows_of_other_half/ppermute | solution.py:219
  55.8 7.6 %collective-permute-start.2 = (s32[4,4,8]{2,1,0:T(4,128)S(1)}, s32[4,4,8]{2,1,0:T(4,128)S(1)}, u32[]{:S(2)}, u32[]{:S(2)}) collective-permute-start(s32[4,4,8]{2,1,0:T(4,128)S(1)} %pad_add_fusion.1), channel_id=1, source_target_pairs={{0,128},{16,144},{32,160},{48,176},{64,192},{80,208},{96,224},{112... | collective-permute-start | bytes 1544 | tf_op jit(solution)/shard_map/tables/ppermute | solution.py:27
  63.4 12.0 %copy-start.24 = (s32[768,8]{0,1:T(8,128)S(1)}, s32[768,8]{0,1:T(8,128)}, u32[]{:S(2)}) copy-start(s32[768,8]{0,1:T(8,128)} %param.8) | copy-start | bytes 73732
  63.5 28.7 %collective-permute-start.18 = (bf16[4,512,128]{2,1,0:T(8,128)(2,1)}, bf16[4,512,128]{2,1,0:T(8,128)(2,1)S(1)}, u32[]{:S(2)}, u32[]{:S(2)}) collective-permute-start(bf16[4,512,128]{2,1,0:T(8,128)(2,1)} %collective-permute-done.17.w), channel_id=1, source_target_pairs={{0,224},{16,240},{32,0},{48,16},{64,32},{80,48},{96,64},{112,80},{... | collective-permute-start | bytes 1572872 | tf_op jit(solution)/shard_map/tiles_round_z/ppermute | solution.py:27
  64.7 28.9 %collective-permute-start.7 = (bf16[4,512,128]{2,1,0:T(8,128)(2,1)}, bf16[4,512,128]{2,1,0:T(8,128)(2,1)S(1)}, u32[]{:S(2)}, u32[]{:S(2)}) collective-permute-start(bf16[4,512,128]{2,1,0:T(8,128)(2,1)} %collective-permute-done.6.w), channel_id=1, source_target_pairs={{0,32},{16,48},{32,64},{48,80},{64,96},{80,112},{96,128},{112,144}... | collective-permute-start | bytes 1572872 | tf_op jit(solution)/shard_map/tiles_round_z/ppermute | solution.py:27
  66.7 2.8 %copy-start = (bf16[768,4096]{1,0:T(8,128)(2,1)S(1)}, bf16[768,4096]{1,0:T(8,128)(2,1)}, u32[]{:S(2)}) copy-start(bf16[768,4096]{1,0:T(8,128)(2,1)} %x3.17) | copy-start | bytes 18874372
  70.3 5.1 %copy-start.15 = (bf16[4,512,128]{2,1,0:T(8,128)(2,1)S(1)}, bf16[4,512,128]{2,1,0:T(8,128)(2,1)}, u32[]{:S(2)}) copy-start(bf16[4,512,128]{2,1,0:T(8,128)(2,1)} %copy-done.14) | copy-start | bytes 1572868
  92.2 13.0 %collective-permute-start.22 = (bf16[2,512,128]{2,1,0:T(8,128)(2,1)S(1)}, bf16[2,512,128]{2,1,0:T(8,128)(2,1)S(1)}, u32[]{:S(2)}, u32[]{:S(2)}) collective-permute-start(bf16[2,512,128]{2,1,0:T(8,128)(2,1)S(1)} %slice.9), channel_id=1, source_target_pairs={{0,224},{16,240},{32,0},{48,16},{64,32},{80,48},{96,64},{112,80},{... | collective-permute-start | bytes 786440 | tf_op jit(solution)/shard_map/tiles_round_z/ppermute | solution.py:27
  93.6 5.4 %copy-start.12 = (bf16[4,512,128]{2,1,0:T(8,128)(2,1)}, bf16[4,512,128]{2,1,0:T(8,128)(2,1)S(1)}, u32[]{:S(2)}) copy-start(bf16[4,512,128]{2,1,0:T(8,128)(2,1)S(1)} %collective-permute-done.7.w) | copy-start | bytes 1572868
  93.6 15.0 %collective-permute-start.8 = (bf16[2,512,128]{2,1,0:T(8,128)(2,1)S(1)}, bf16[2,512,128]{2,1,0:T(8,128)(2,1)S(1)}, u32[]{:S(2)}, u32[]{:S(2)}) collective-permute-start(bf16[2,512,128]{2,1,0:T(8,128)(2,1)S(1)} %slice.8), channel_id=1, source_target_pairs={{0,32},{16,48},{32,64},{48,80},{64,96},{80,112},{96,128},{112,144}... | collective-permute-start | bytes 786440 | tf_op jit(solution)/shard_map/tiles_round_z/ppermute | solution.py:27
  105.2 2.5 %copy-start.25 = (bf16[2,512,128]{2,1,0:T(8,128)(2,1)}, bf16[2,512,128]{2,1,0:T(8,128)(2,1)S(1)}, u32[]{:S(2)}) copy-start(bf16[2,512,128]{2,1,0:T(8,128)(2,1)S(1)} %collective-permute-done.22.w) | copy-start | bytes 786436
  111.9 2.8 %copy-start.1 = (bf16[768,4096]{1,0:T(8,128)(2,1)S(1)}, bf16[768,4096]{1,0:T(8,128)(2,1)}, u32[]{:S(2)}) copy-start(bf16[768,4096]{1,0:T(8,128)(2,1)} %all-gather.2.cloned.1.call-done.x0.x1.x2.x3) | copy-start | bytes 18874372
  116.6 4.7 %copy-start.2 = (bf16[768,4096]{1,0:T(8,128)(2,1)S(1)}, bf16[768,4096]{1,0:T(8,128)(2,1)}, u32[]{:S(2)}) copy-start(bf16[768,4096]{1,0:T(8,128)(2,1)} %all-gather.2.cloned.1.call-done.x0.x1.x2.x3) | copy-start | bytes 18874372
  116.6 4.7 %copy-start.20 = (f32[2,128,512]{2,1,0:T(8,128)S(1)}, f32[2,128,512]{2,1,0:T(8,128)}, u32[]{:S(2)}) copy-start(f32[2,128,512]{2,1,0:T(8,128)} %copy-done.19) | copy-start | bytes 1572868
  119.3 6.0 %copy-start.10 = (f32[4,128,512]{2,1,0:T(8,128)S(1)}, f32[4,128,512]{2,1,0:T(8,128)}, u32[]{:S(2)}) copy-start(f32[4,128,512]{2,1,0:T(8,128)} %copy-done.9) | copy-start | bytes 3145732
  119.3 6.0 %copy-start.13 = (bf16[4,512,128]{2,1,0:T(8,128)(2,1)S(1)}, bf16[4,512,128]{2,1,0:T(8,128)(2,1)}, u32[]{:S(2)}) copy-start(bf16[4,512,128]{2,1,0:T(8,128)(2,1)} %copy-done.12) | copy-start | bytes 1572868
  119.3 19.9 %collective-permute-start.23 = (s16[272,512]{1,0:T(8,128)(2,1)S(1)}, s16[272,512]{1,0:T(8,128)(2,1)S(1)}, u32[]{:S(2)}, u32[]{:S(2)}) collective-permute-start(s16[272,512]{1,0:T(8,128)(2,1)S(1)} %encode.24), channel_id=1, source_target_pairs={{0,32},{16,48},{32,64},{48,80},{64,96},{80,112},{96,128},{112,144}... | collective-permute-start | bytes 835592 | tf_op jit(solution)/shard_map/sums_round_z/ppermute | solution.py:27
  123.9 7.2 %copy-start.8 = (f32[4,128,512]{2,1,0:T(8,128)S(1)}, f32[4,128,512]{2,1,0:T(8,128)}, u32[]{:S(2)}) copy-start(f32[4,128,512]{2,1,0:T(8,128)} %copy-done.7) | copy-start | bytes 3145732
  123.9 12.5 %collective-permute-start.9 = (s16[272,512]{1,0:T(8,128)(2,1)S(1)}, s16[272,512]{1,0:T(8,128)(2,1)S(1)}, u32[]{:S(2)}, u32[]{:S(2)}) collective-permute-start(s16[272,512]{1,0:T(8,128)(2,1)S(1)} %encode.14), channel_id=1, source_target_pairs={{0,224},{16,240},{32,0},{48,16},{64,32},{80,48},{96,64},{112,80},{... | collective-permute-start | bytes 835592 | tf_op jit(solution)/shard_map/sums_round_z/ppermute | solution.py:27
  129.7 9.9 %copy-start.6 = (f32[4,128,512]{2,1,0:T(8,128)S(1)}, f32[4,128,512]{2,1,0:T(8,128)}, u32[]{:S(2)}) copy-start(f32[4,128,512]{2,1,0:T(8,128)} %copy-done.5) | copy-start | bytes 3145732
  129.7 20.5 %collective-permute-start.13 = (s16[272,512]{1,0:T(8,128)(2,1)S(1)}, s16[272,512]{1,0:T(8,128)(2,1)S(1)}, u32[]{:S(2)}, u32[]{:S(2)}) collective-permute-start(s16[272,512]{1,0:T(8,128)(2,1)S(1)} %encode.18), channel_id=1, source_target_pairs={{0,224},{16,240},{32,0},{48,16},{64,32},{80,48},{96,64},{112,80},{... | collective-permute-start | bytes 835592 | tf_op jit(solution)/shard_map/sums_round_z/ppermute | solution.py:27
  135.6 18.1 %collective-permute-start.19 = (s16[272,512]{1,0:T(8,128)(2,1)S(1)}, s16[272,512]{1,0:T(8,128)(2,1)S(1)}, u32[]{:S(2)}, u32[]{:S(2)}) collective-permute-start(s16[272,512]{1,0:T(8,128)(2,1)S(1)} %encode.21), channel_id=1, source_target_pairs={{0,32},{16,48},{32,64},{48,80},{64,96},{80,112},{96,128},{112,144}... | collective-permute-start | bytes 835592 | tf_op jit(solution)/shard_map/sums_round_z/ppermute | solution.py:27
  136.6 17.4 %collective-permute-start.10 = (s16[272,512]{1,0:T(8,128)(2,1)S(1)}, s16[272,512]{1,0:T(8,128)(2,1)S(1)}, u32[]{:S(2)}, u32[]{:S(2)}) collective-permute-start(s16[272,512]{1,0:T(8,128)(2,1)S(1)} %encode.15), channel_id=1, source_target_pairs={{0,224},{16,240},{32,0},{48,16},{64,32},{80,48},{96,64},{112,80},{... | collective-permute-start | bytes 835592 | tf_op jit(solution)/shard_map/sums_round_z/ppermute | solution.py:27
  139.3 5.6 %copy-start.4 = (f32[4,128,512]{2,1,0:T(8,128)S(1)}, f32[4,128,512]{2,1,0:T(8,128)}, u32[]{:S(2)}) copy-start(f32[4,128,512]{2,1,0:T(8,128)} %copy-done.3) | copy-start | bytes 3145732
  139.3 18.1 %collective-permute-start.24 = (s16[272,512]{1,0:T(8,128)(2,1)S(1)}, s16[272,512]{1,0:T(8,128)(2,1)S(1)}, u32[]{:S(2)}, u32[]{:S(2)}) collective-permute-start(s16[272,512]{1,0:T(8,128)(2,1)S(1)} %encode.25), channel_id=1, source_target_pairs={{0,32},{16,48},{32,64},{48,80},{64,96},{80,112},{96,128},{112,144}... | collective-permute-start | bytes 835592 | tf_op jit(solution)/shard_map/sums_round_z/ppermute | solution.py:27
  150.2 7.5 %copy-start.18 = (bf16[4,512,128]{2,1,0:T(8,128)(2,1)S(1)}, bf16[4,512,128]{2,1,0:T(8,128)(2,1)}, u32[]{:S(2)}) copy-start(bf16[4,512,128]{2,1,0:T(8,128)(2,1)} %copy-done.17) | copy-start | bytes 1572868
  150.4 16.1 %collective-permute-start.14 = (s16[272,512]{1,0:T(8,128)(2,1)S(1)}, s16[272,512]{1,0:T(8,128)(2,1)S(1)}, u32[]{:S(2)}, u32[]{:S(2)}) collective-permute-start(s16[272,512]{1,0:T(8,128)(2,1)S(1)} %encode.19), channel_id=1, source_target_pairs={{0,224},{16,240},{32,0},{48,16},{64,32},{80,48},{96,64},{112,80},{... | collective-permute-start | bytes 835592 | tf_op jit(solution)/shard_map/sums_round_z/ppermute | solution.py:27
  153.9 16.2 %collective-permute-start.20 = (s16[272,512]{1,0:T(8,128)(2,1)S(1)}, s16[272,512]{1,0:T(8,128)(2,1)S(1)}, u32[]{:S(2)}, u32[]{:S(2)}) collective-permute-start(s16[272,512]{1,0:T(8,128)(2,1)S(1)} %encode.22), channel_id=1, source_target_pairs={{0,32},{16,48},{32,64},{48,80},{64,96},{80,112},{96,128},{112,144}... | collective-permute-start | bytes 835592 | tf_op jit(solution)/shard_map/sums_round_z/ppermute | solution.py:27
  154.2 16.2 %collective-permute-start.11 = (s16[272,512]{1,0:T(8,128)(2,1)S(1)}, s16[272,512]{1,0:T(8,128)(2,1)S(1)}, u32[]{:S(2)}, u32[]{:S(2)}) collective-permute-start(s16[272,512]{1,0:T(8,128)(2,1)S(1)} %encode.16), channel_id=1, source_target_pairs={{0,224},{16,240},{32,0},{48,16},{64,32},{80,48},{96,64},{112,80},{... | collective-permute-start | bytes 835592 | tf_op jit(solution)/shard_map/sums_round_z/ppermute | solution.py:27
  157.6 4.5 %copy-start.16 = (bf16[4,512,128]{2,1,0:T(8,128)(2,1)S(1)}, bf16[4,512,128]{2,1,0:T(8,128)(2,1)}, u32[]{:S(2)}) copy-start(bf16[4,512,128]{2,1,0:T(8,128)(2,1)} %copy-done.14) | copy-start | bytes 1572868
  157.6 16.2 %collective-permute-start.25 = (s16[272,512]{1,0:T(8,128)(2,1)S(1)}, s16[272,512]{1,0:T(8,128)(2,1)S(1)}, u32[]{:S(2)}, u32[]{:S(2)}) collective-permute-start(s16[272,512]{1,0:T(8,128)(2,1)S(1)} %encode.26), channel_id=1, source_target_pairs={{0,32},{16,48},{32,64},{48,80},{64,96},{80,112},{96,128},{112,144}... | collective-permute-start | bytes 835592 | tf_op jit(solution)/shard_map/sums_round_z/ppermute | solution.py:27
  157.7 16.3 %slice-start = ((s8[6291456]{0:T(1024)(128)(4,1)}), s8[4194304]{0:T(1024)(128)(4,1)S(1)}, s32[]{:S(2)}) async-start(s8[6291456]{0:T(1024)(128)(4,1)} %bitcast.5), calls=%async_computation.1 | async-start | bytes 8388608
  162.1 12.0 %slice-start.1 = ((s8[6291456]{0:T(1024)(128)(4,1)}), s8[2097152]{0:T(1024)(128)(4,1)S(1)}, s32[]{:S(2)}) async-start(s8[6291456]{0:T(1024)(128)(4,1)} %bitcast.5), calls=%async_computation.2 | async-start | bytes 4194304
  166.7 16.2 %collective-permute-start.15 = (s16[272,512]{1,0:T(8,128)(2,1)S(1)}, s16[272,512]{1,0:T(8,128)(2,1)S(1)}, u32[]{:S(2)}, u32[]{:S(2)}) collective-permute-start(s16[272,512]{1,0:T(8,128)(2,1)S(1)} %encode.20), channel_id=1, source_target_pairs={{0,224},{16,240},{32,0},{48,16},{64,32},{80,48},{96,64},{112,80},{... | collective-permute-start | bytes 835592 | tf_op jit(solution)/shard_map/sums_round_z/ppermute | solution.py:27
  170.2 12.7 %collective-permute-start.21 = (s16[272,512]{1,0:T(8,128)(2,1)S(1)}, s16[272,512]{1,0:T(8,128)(2,1)S(1)}, u32[]{:S(2)}, u32[]{:S(2)}) collective-permute-start(s16[272,512]{1,0:T(8,128)(2,1)S(1)} %encode.23), channel_id=1, source_target_pairs={{0,32},{16,48},{32,64},{48,80},{64,96},{80,112},{96,128},{112,144}... | collective-permute-start | bytes 835592 | tf_op jit(solution)/shard_map/sums_round_z/ppermute | solution.py:27
  170.5 12.4 %collective-permute-start.12 = (s16[272,512]{1,0:T(8,128)(2,1)S(1)}, s16[272,512]{1,0:T(8,128)(2,1)S(1)}, u32[]{:S(2)}, u32[]{:S(2)}) collective-permute-start(s16[272,512]{1,0:T(8,128)(2,1)S(1)} %encode.17), channel_id=1, source_target_pairs={{0,224},{16,240},{32,0},{48,16},{64,32},{80,48},{96,64},{112,80},{... | collective-permute-start | bytes 835592 | tf_op jit(solution)/shard_map/sums_round_z/ppermute | solution.py:27
  174.0 9.0 %collective-permute-start.26 = (s16[272,512]{1,0:T(8,128)(2,1)S(1)}, s16[272,512]{1,0:T(8,128)(2,1)S(1)}, u32[]{:S(2)}, u32[]{:S(2)}) collective-permute-start(s16[272,512]{1,0:T(8,128)(2,1)S(1)} %encode.27), channel_id=1, source_target_pairs={{0,32},{16,48},{32,64},{48,80},{64,96},{80,112},{96,128},{112,144}... | collective-permute-start | bytes 835592 | tf_op jit(solution)/shard_map/sums_round_z/ppermute | solution.py:27
  178.5 4.5 %copy-start.11 = (f32[4,4,128,128]{3,2,1,0:T(8,128)S(1)}, f32[4,4,128,128]{3,2,1,0:T(8,128)}, u32[]{:S(2)}) copy-start(f32[4,4,128,128]{3,2,1,0:T(8,128)} %weight.1) | copy-start | bytes 3145732
  178.5 4.5 %copy-start.27 = (f32[4,4,128,128]{3,2,1,0:T(8,128)S(1)}, f32[4,4,128,128]{3,2,1,0:T(8,128)}, u32[]{:S(2)}) copy-start(f32[4,4,128,128]{3,2,1,0:T(8,128)} %first.1) | copy-start | bytes 3145732
  178.5 4.5 %copy-start.28 = (f32[4,4,128,128]{3,2,1,0:T(8,128)S(1)}, f32[4,4,128,128]{3,2,1,0:T(8,128)}, u32[]{:S(2)}) copy-start(f32[4,4,128,128]{3,2,1,0:T(8,128)} %second.1) | copy-start | bytes 3145732
  (12 other events, 10.6 us)
Sparse Core Ops, SparseCore 0:
  21.3 47.0 all-gather.1
